TPU v7x, 128 devices: a whole 4x4x4 slice. The times are simulated.
128 devices in a mesh: row: 8 (over z_hi, x), col: 16 (over z_lo, y, core).
Axes of the slice: x: 4, y: 4, z: 4 (z_hi: 2, z_lo: 2; z = z_hi * 2 + z_lo), core: 2. Of those that a mesh axis runs over, the one named last changes fastest.
Arguments:
- subspace: bfloat16 [65536, 128], P(('row', 'col')), may hold values from -6 to 6
- blocks: bfloat16 [8, 16, 512, 128, 128], P('row', 'col'), may hold values from -0.0625 to 0.0625
- row_pointer: int32 [8, 16, 65], P('row', 'col'), may hold values from 0 to 512, as said below
- block_column: int32 [8, 16, 512], P('row', 'col'), may hold values from 0 to 31, as said below
Outputs:
- filtered: float32 [65536, 128], P(('row', 'col'))
Inputs may be any that keep to these rules, and one draw needn't show every extreme that they name: `row_pointer`: each tile's pointers start at 0 and rise by 1 to 12 a block row; a tile's last pointer, its count of live blocks, is 128 or 512, and some tile holds 512 in every draw. `block_column`: local block columns are distinct within a block row; slots beyond a tile's count hold 0.
All inputs are finite; a program needn't handle non-finite values.
Results may differ from a plain program's by a relative error of at most 0.003.
Values may be sent and summed in bfloat16 or wider, within the bound.
No kernel may reach another device: no remote copies, remote signals or barrier semaphores. Data moves between devices by JAX's collectives and lax.ppermute only.
A program may use at most 128 MiB of HBM per device.

v0:
```python
import functools

import jax
import jax.numpy as jnp
from jax import lax
from jax.experimental import pallas as pl
from jax.experimental.pallas import tpu as pltpu
from jax.sharding import PartitionSpec as P

UNROLL = 24
PARTS = 16
MOST = 12
MIB = 1024 * 1024


def pair_list(core_ref, pointer_ref, column_ref, word_ref, count_ref, *, groups, height):
    core = core_ref[0]
    for half in range(2):
        which = core if half else 1 - core

        def one_row(local, number):
            row = (2 * (local // height) + which) * height + local % height
            first, last = pointer_ref[row], pointer_ref[row + 1]

            def one_pair(k, _):
                j = first + 2 * k
                both = (j + 1 < last).astype(jnp.int32)
                word_ref[half, number + k] = (
                    j + local * 512 + column_ref[j] * 16384 + column_ref[j + both] * 524288 + (1 + both) * 16777216
                )
                return 0

            pairs = (last - first + 1) // 2
            lax.fori_loop(0, pairs, one_pair, 0)
            return number + pairs

        total = lax.fori_loop(0, groups * height, one_row, 0)
        for k in range(UNROLL):
            word_ref[half, total + k] = word_ref[half, total - 1] & 16383
        count_ref[half] = (total + UNROLL - 1) // UNROLL


def make_lists(core, pointer, columns, height):
    rows = pointer.shape[0] - 1
    groups = rows // height // 2
    smem = pl.BlockSpec(memory_space=pltpu.SMEM)
    width = (rows // 2) * (MOST // 2) + UNROLL
    return pl.pallas_call(
        functools.partial(pair_list, groups=groups, height=height),
        in_specs=[smem] * 3,
        out_specs=[smem] * 2,
        out_shape=[jax.ShapeDtypeStruct((2, width), jnp.int32), jax.ShapeDtypeStruct((2,), jnp.int32)],
        compiler_params=pltpu.CompilerParams(vmem_limit_bytes=2 * MIB),
        name="pair_list",
    )(core, pointer, columns)


def add_pairs(word_ref, count_ref, vector_ref, block_ref, out_ref, half, ready, arrive):
    out_ref[...] = jnp.zeros_like(out_ref)

    def body(step, ready):
        ready = arrive((word_ref[half, step * UNROLL + UNROLL - 1] & 511) + 1, ready)
        for k in range(UNROLL):
            word = word_ref[half, step * UNROLL + k]
            j = word & 511
            row = (word >> 9) & 31
            c1 = (word >> 14) & 31
            c2 = (word >> 19) & 31
            n = word >> 24
            left = jnp.concatenate([block_ref[j], block_ref[j + (n >> 1)]], axis=1)
            v1 = vector_ref[c1]
            v2 = vector_ref[c2]
            right = jnp.concatenate([jnp.where(n > 0, v1, jnp.zeros_like(v1)), jnp.where(n > 1, v2, jnp.zeros_like(v2))], axis=0)
            out_ref[row] += jnp.dot(left, right, preferred_element_type=jnp.float32)
        return ready

    return lax.fori_loop(0, count_ref[half], body, ready)


def given_kernel(pointer_ref, word_ref, count_ref, vector_ref, source_ref, out_ref, block_ref, sem):
    step = source_ref.shape[0] // PARTS
    used = (pointer_ref[pointer_ref.shape[0] - 1] + step - 1) // step

    def copy(k):
        part = pl.ds(k * step, step)
        return pltpu.make_async_copy(source_ref.at[part], block_ref.at[part], sem.at[k])

    def start(k, _):
        copy(k).start()
        return 0

    def wait(k, _):
        copy(k).wait()
        return 0

    def arrive(last, ready):
        needed = jnp.maximum(jnp.minimum(last // step + 1, used), ready)
        lax.fori_loop(ready, needed, wait, 0)
        return needed

    lax.fori_loop(0, used, start, 0)
    ready = add_pairs(word_ref, count_ref, vector_ref, block_ref, out_ref, 0, 0, arrive)
    lax.fori_loop(ready, used, wait, 0)


def half_kernel(word_ref, count_ref, vector_ref, block_ref, out_ref, *, half):
    add_pairs(word_ref, count_ref, vector_ref, block_ref, out_ref, half, 0, lambda last, ready: ready)


def given_terms(pointer, words, counts, vector, tile_blocks):
    smem = pl.BlockSpec(memory_space=pltpu.SMEM)
    vmem = pl.BlockSpec(memory_space=pltpu.VMEM)
    return pl.pallas_call(
        given_kernel,
        in_specs=[smem, smem, smem, vmem, pl.BlockSpec(memory_space=pl.ANY)],
        out_specs=[vmem, vmem],
        out_shape=[
            jax.ShapeDtypeStruct((vector.shape[0], tile_blocks.shape[1], vector.shape[2]), jnp.float32),
            pltpu.VMEM(tile_blocks.shape, tile_blocks.dtype),
        ],
        scratch_shapes=[pltpu.SemaphoreType.DMA((PARTS,))],
        compiler_params=pltpu.CompilerParams(vmem_limit_bytes=24 * MIB),
        name="given_terms",
    )(pointer, words, counts, vector, pltpu.with_memory_space_constraint(tile_blocks, pltpu.HBM))


def half_terms(words, counts, vector, held, half):
    smem = pl.BlockSpec(memory_space=pltpu.SMEM)
    vmem = pl.BlockSpec(memory_space=pltpu.VMEM)
    return pl.pallas_call(
        functools.partial(half_kernel, half=half),
        in_specs=[smem, smem, vmem, vmem],
        out_specs=vmem,
        out_shape=jax.ShapeDtypeStruct((vector.shape[0], held.shape[1], vector.shape[2]), jnp.float32),
        compiler_params=pltpu.CompilerParams(vmem_limit_bytes=24 * MIB),
        name="half_terms",
    )(words, counts, vector, pltpu.with_memory_space_constraint(held, pltpu.VMEM))


def combine_kernel(kept_ref, taken_ref, out_ref):
    chips, taller, width = out_ref.shape
    rows, size, _ = kept_ref.shape
    height = rows // chips
    step = 32
    tops = []
    for chip in range(chips):
        most = jnp.zeros((step, width), jnp.float32)
        for k in range(height):
            row = chip * height + k
            for t in range(0, size, step):
                both = kept_ref[row, t : t + step] + taken_ref[row, t : t + step]
                out_ref[chip, k * size + t : k * size + t + step] = both
                most = jnp.maximum(most, jnp.abs(both))
        tops.append(jnp.max(most, axis=0, keepdims=True))
    most = jnp.max(jnp.concatenate(tops, axis=0), axis=1, keepdims=True)
    power = jnp.floor(jnp.log2(jnp.maximum(most, 1e-30))) - 14.0
    power = jnp.broadcast_to(power, (chips, width))
    scale = jnp.exp2(-power)
    for chip in range(chips):
        by = jnp.broadcast_to(scale[chip : chip + 1], (step, width))
        for t in range(0, height * size, step):
            out_ref[chip, t : t + step] = out_ref[chip, t : t + step] * by
        out_ref[chip, height * size :] = jnp.broadcast_to(power[chip : chip + 1], (taller - height * size, width))


def combine(kept, taken, chips):
    vmem = pl.BlockSpec(memory_space=pltpu.VMEM)
    rows, size, width = kept.shape
    return pl.pallas_call(
        combine_kernel,
        in_specs=[vmem, vmem],
        out_specs=vmem,
        out_shape=jax.ShapeDtypeStruct((chips, rows // chips * size + 8, width), jnp.float32),
        compiler_params=pltpu.CompilerParams(vmem_limit_bytes=24 * MIB),
        name="combine",
    )(kept, taken)


def per_device(subspace, blocks, row_pointer, block_column):
    tile_blocks = blocks[0, 0]
    pointer = row_pointer[0, 0]
    size = tile_blocks.shape[1]
    own_rows, width = subspace.shape
    height = own_rows // size
    chips = lax.axis_size("col") // 2
    core = lax.axis_index("col") % 2
    swap = [(c, c ^ 1) for c in range(2 * chips)]
    alike = [[2 * d + k for d in range(chips)] for k in range(2)]
    sources = lax.axis_size("row")
    words, counts = make_lists(core.reshape(1), pointer, block_column[0, 0], height)

    def multiply(vector, held):
        spread = jnp.broadcast_to(vector[None], (sources, own_rows, width))
        gathered = lax.all_to_all(spread, "row", 0, 0).reshape(-1, size, width)
        if held is None:
            given, held = given_terms(pointer, words, counts, gathered, tile_blocks)
        else:
            given = half_terms(words, counts, gathered, held, 0)
        taken = lax.ppermute(given, "col", swap)
        kept = half_terms(words, counts, gathered, held, 1)
        scaled = combine(kept, taken, chips).astype(jnp.float16)
        parts = lax.all_to_all(scaled, "col", 0, 0, axis_index_groups=alike)
        weight = jnp.exp2(parts[:, own_rows : own_rows + 1, :1].astype(jnp.float32))
        return jnp.sum(parts[:, :own_rows].astype(jnp.float32) * weight, axis=0), held

    total, held = multiply(subspace, None)
    first = total.astype(jnp.bfloat16)
    total, held = multiply(first, held)
    second = (2.0 * total - subspace.astype(jnp.float32)).astype(jnp.bfloat16)
    total, held = multiply(second, held)
    return 2.0 * total - first.astype(jnp.float32)


def solution(mesh):
    placed = (
        P(("row", "col"), None),
        P("row", "col", None, None, None),
        P("row", "col", None),
        P("row", "col", None),
    )
    return jax.shard_map(
        per_device, mesh=mesh, in_specs=placed, out_specs=P(("row", "col"), None), check_vma=False
    )
```

profile of v0, /device:TPU:6, one launch (start us, length us, event | category | flops | bytes accessed | tf_op | source)
XLA Modules:
  0.0 154.6 jit_solution(14506335580844359144)
XLA Ops:
  0.0 0.0 copy-start.1
  0.0 0.0 copy-start
  0.0 2.1 %broadcast_in_dim.6 = bf16[8,512,128]{2,1,0:T(8,128)(2,1)} broadcast(bf16[512,128]{1,0:T(8,128)(2,1)} %param.4), dimensions={1,2} | broadcast | bytes 1179648 | tf_op jit(solution)/shard_map/broadcast_in_dim | solution.py:193
  2.1 8.1 %all-to-all-start = ((bf16[8,512,128]{2,1,0:T(8,128)(2,1)}), bf16[8,512,128]{2,1,0:T(8,128)(2,1)S(1)}, u32[]{:S(2)}, u32[]{:S(2)}) async-start(bf16[8,512,128]{2,1,0:T(8,128)(2,1)} %broadcast_in_dim.6), calls=%async_computation | async-start | bytes 2097152 | tf_op jit(solution)/shard_map/all_to_all | solution.py:194
  10.1 0.0 copy-done.1
  10.2 0.0 copy-done
  10.2 4.0 %pair_list.1 = (s32[2,216]{1,0:T(2,128)S(1)}, s32[2]{0:T(128)S(1)}) custom-call(s32[1]{0:T(128)} %bitcast.core_ref, s32[65]{0:T(128)S(1)} %bitcast.13, s32[512]{0:T(512)S(1)} %bitcast.15), custom_call_target="tpu_custom_call" | custom-call | tf_op jit(solution)/shard_map/pair_list/pallas_call | solution.py:48
  14.1 10.5 %all-to-all-done = bf16[8,512,128]{2,1,0:T(8,128)(2,1)S(1)} async-done(((bf16[8,512,128]{2,1,0:T(8,128)(2,1)}), bf16[8,512,128]{2,1,0:T(8,128)(2,1)S(1)}, u32[]{:S(2)}, u32[]{:S(2)}) %all-to-all-start) | async-done | bytes 1048608 | tf_op jit(solution)/shard_map/all_to_all | solution.py:194
  24.7 3.9 %given_terms.1 = (f32[32,128,128]{2,1,0:T(8,128)S(1)}, bf16[512,128,128]{2,1,0:T(8,128)(2,1)S(1)}) custom-call(s32[65]{0:T(128)S(1)} %bitcast.14, s32[2,216]{1,0:T(2,128)S(1)} %get-tuple-element.9.word_ref, s32[2]{0:T(128)S(1)} %get-tuple-element.10.count_ref, bf16[32,128,128]{2,1,0:T(8,128)(2,1)S(1)} %bitcast.7, bf16[512,128,128]{2,1,0:T(8,128)(2,1)} %bitcast.16), custom_call_target="tpu_custom_call" | custom-call | tf_op jit(solution)/shard_map/given_terms/pallas_call | solution.py:113
  28.5 3.8 %collective-permute-start = (f32[32,128,128]{2,1,0:T(8,128)S(1)}, f32[32,128,128]{2,1,0:T(8,128)S(1)}, u32[]{:S(2)}, u32[]{:S(2)}) collective-permute-start(f32[32,128,128]{2,1,0:T(8,128)S(1)} %get-tuple-element.12), channel_id=1, source_target_pairs={{0,1},{1,0},{2,3},{3,2},{4,5},{5,4},{6,7},{7,6},{8,9},{9,8},{10,11... | collective-permute-start | bytes 6291464 | tf_op jit(solution)/shard_map/ppermute | solution.py:199
  32.3 2.0 %half_terms.5.kept_ref = f32[32,128,128]{2,1,0:T(8,128)S(1)} custom-call(s32[2,216]{1,0:T(2,128)S(1)} %get-tuple-element.9.word_ref, s32[2]{0:T(128)S(1)} %get-tuple-element.10.count_ref, bf16[32,128,128]{2,1,0:T(8,128)(2,1)S(1)} %bitcast.8, bf16[512,128,128]{2,1,0:T(8,128)(2,1)S(1)} %get-tuple-element.11.block_ref), custom_call_target="tpu_custom_call" | custom-call | tf_op jit(solution)/shard_map/half_terms/pallas_call | solution.py:130
  34.3 1.8 %collective-permute-done.taken_ref = f32[32,128,128]{2,1,0:T(8,128)S(1)} collective-permute-done((f32[32,128,128]{2,1,0:T(8,128)S(1)}, f32[32,128,128]{2,1,0:T(8,128)S(1)}, u32[]{:S(2)}, u32[]{:S(2)}) %collective-permute-start) | collective-permute-done | bytes 2097184 | tf_op jit(solution)/shard_map/ppermute | solution.py:199
  36.1 0.5 combine.3
  36.6 0.1 convert_element_type.43
  36.7 21.3 %all_to_all.30 = f16[8,520,128]{2,1,0:T(8,128)(2,1)S(1)} all-to-all(f16[8,520,128]{2,1,0:T(8,128)(2,1)S(1)} %convert_element_type.43), channel_id=1, replica_groups={{0,2,4,6,8,10,12,14},{1,3,5,7,9,11,13,15},{16,18,20,22,24,26,28,30},{17..., dimensions={0} | all-to-all | bytes 2129920 | tf_op jit(solution)/shard_map/all_to_all | solution.py:202
  58.0 0.1 fusion.6
  58.2 0.3 multiply_reduce_fusion.2
  58.4 0.1 broadcast_in_dim.7
  58.6 20.2 %all_to_all.31 = bf16[8,512,128]{2,1,0:T(8,128)(2,1)S(1)} all-to-all(bf16[8,512,128]{2,1,0:T(8,128)(2,1)S(1)} %broadcast_in_dim.7), channel_id=1, replica_groups=mesh['row'=8,'col'=16] {'row'}, dimensions={0} | all-to-all | bytes 2097152 | tf_op jit(solution)/shard_map/all_to_all | solution.py:194
  78.8 1.9 %half_terms.7 = f32[32,128,128]{2,1,0:T(8,128)S(1)} custom-call(s32[2,216]{1,0:T(2,128)S(1)} %get-tuple-element.9.word_ref, s32[2]{0:T(128)S(1)} %get-tuple-element.10.count_ref, bf16[32,128,128]{2,1,0:T(8,128)(2,1)S(1)} %bitcast.11, bf16[512,128,128]{2,1,0:T(8,128)(2,1)S(1)} %get-tuple-element.11.block_ref), custom_call_target="tpu_custom_call" | custom-call | tf_op jit(solution)/shard_map/half_terms/pallas_call | solution.py:130
  80.8 0.6 collective-permute-start.1
  81.4 2.0 %half_terms.6.kept_ref = f32[32,128,128]{2,1,0:T(8,128)S(1)} custom-call(s32[2,216]{1,0:T(2,128)S(1)} %get-tuple-element.9.word_ref, s32[2]{0:T(128)S(1)} %get-tuple-element.10.count_ref, bf16[32,128,128]{2,1,0:T(8,128)(2,1)S(1)} %bitcast.12, bf16[512,128,128]{2,1,0:T(8,128)(2,1)S(1)} %get-tuple-element.11.block_ref), custom_call_target="tpu_custom_call" | custom-call | tf_op jit(solution)/shard_map/half_terms/pallas_call | solution.py:130
  83.4 1.8 %collective-permute-done.1.taken_ref = f32[32,128,128]{2,1,0:T(8,128)S(1)} collective-permute-done((f32[32,128,128]{2,1,0:T(8,128)S(1)}, f32[32,128,128]{2,1,0:T(8,128)S(1)}, u32[]{:S(2)}, u32[]{:S(2)}) %collective-permute-start.1) | collective-permute-done | bytes 2097184 | tf_op jit(solution)/shard_map/ppermute | solution.py:199
  85.2 0.5 combine.4
  85.7 0.1 convert_element_type.47
  85.8 0.0 copy-start.2
  85.8 20.8 %all_to_all.32 = f16[8,520,128]{2,1,0:T(8,128)(2,1)S(1)} all-to-all(f16[8,520,128]{2,1,0:T(8,128)(2,1)S(1)} %convert_element_type.47), channel_id=1, replica_groups={{0,2,4,6,8,10,12,14},{1,3,5,7,9,11,13,15},{16,18,20,22,24,26,28,30},{17..., dimensions={0} | all-to-all | bytes 2129920 | tf_op jit(solution)/shard_map/all_to_all | solution.py:202
  106.6 0.1 fusion.7
  106.8 0.3 multiply_reduce_fusion.1
  107.0 0.0 copy-done.2
  107.1 0.1 broadcast_in_dim.8
  107.2 18.7 %all_to_all.33 = bf16[8,512,128]{2,1,0:T(8,128)(2,1)S(1)} all-to-all(bf16[8,512,128]{2,1,0:T(8,128)(2,1)S(1)} %broadcast_in_dim.8), channel_id=1, replica_groups=mesh['row'=8,'col'=16] {'row'}, dimensions={0} | all-to-all | bytes 2097152 | tf_op jit(solution)/shard_map/all_to_all | solution.py:194
  126.0 1.9 %half_terms.9 = f32[32,128,128]{2,1,0:T(8,128)S(1)} custom-call(s32[2,216]{1,0:T(2,128)S(1)} %get-tuple-element.9.word_ref, s32[2]{0:T(128)S(1)} %get-tuple-element.10.count_ref, bf16[32,128,128]{2,1,0:T(8,128)(2,1)S(1)} %bitcast.9, bf16[512,128,128]{2,1,0:T(8,128)(2,1)S(1)} %get-tuple-element.11.block_ref), custom_call_target="tpu_custom_call" | custom-call | tf_op jit(solution)/shard_map/half_terms/pallas_call | solution.py:130
  127.9 0.1 collective-permute-start.2
  128.0 2.0 %half_terms.8.kept_ref = f32[32,128,128]{2,1,0:T(8,128)S(1)} custom-call(s32[2,216]{1,0:T(2,128)S(1)} %get-tuple-element.9.word_ref, s32[2]{0:T(128)S(1)} %get-tuple-element.10.count_ref, bf16[32,128,128]{2,1,0:T(8,128)(2,1)S(1)} %bitcast.10, bf16[512,128,128]{2,1,0:T(8,128)(2,1)S(1)} %get-tuple-element.11.block_ref), custom_call_target="tpu_custom_call" | custom-call | tf_op jit(solution)/shard_map/half_terms/pallas_call | solution.py:130
  129.9 2.2 %collective-permute-done.2.taken_ref = f32[32,128,128]{2,1,0:T(8,128)S(1)} collective-permute-done((f32[32,128,128]{2,1,0:T(8,128)S(1)}, f32[32,128,128]{2,1,0:T(8,128)S(1)}, u32[]{:S(2)}, u32[]{:S(2)}) %collective-permute-start.2) | collective-permute-done | bytes 2097184 | tf_op jit(solution)/shard_map/ppermute | solution.py:199
  132.1 0.5 combine.5
  132.6 0.1 convert_element_type.52
  132.7 20.7 %all_to_all.34 = f16[8,520,128]{2,1,0:T(8,128)(2,1)S(1)} all-to-all(f16[8,520,128]{2,1,0:T(8,128)(2,1)S(1)} %convert_element_type.52), channel_id=1, replica_groups={{0,2,4,6,8,10,12,14},{1,3,5,7,9,11,13,15},{16,18,20,22,24,26,28,30},{17..., dimensions={0} | all-to-all | bytes 2129920 | tf_op jit(solution)/shard_map/all_to_all | solution.py:202
  153.5 0.1 fusion.8
  153.6 0.3 multiply_reduce_fusion
  153.9 0.7 convert_subtract_fusion
  (1 shorter events, 0.0 us)
Async XLA Ops:
  0.0 10.1 %copy-start.1 = (s32[1,1,512]{2,1,0:T(1,128)S(1)}, s32[1,1,512]{2,1,0:T(1,128)}, u32[]{:S(2)}) copy-start(s32[1,1,512]{2,1,0:T(1,128)} %param.7) | copy-start | bytes 6148
  0.0 10.2 %copy-start = (s32[1,1,65]{2,1,0:T(1,128)S(1)}, s32[1,1,65]{2,1,0:T(1,128)}, u32[]{:S(2)}) copy-start(s32[1,1,65]{2,1,0:T(1,128)} %param.6) | copy-start | bytes 784
  2.1 22.6 %all-to-all-start = ((bf16[8,512,128]{2,1,0:T(8,128)(2,1)}), bf16[8,512,128]{2,1,0:T(8,128)(2,1)S(1)}, u32[]{:S(2)}, u32[]{:S(2)}) async-start(bf16[8,512,128]{2,1,0:T(8,128)(2,1)} %broadcast_in_dim.6), calls=%async_computation | async-start | bytes 2097152 | tf_op jit(solution)/shard_map/all_to_all | solution.py:194
  28.5 7.5 %collective-permute-start = (f32[32,128,128]{2,1,0:T(8,128)S(1)}, f32[32,128,128]{2,1,0:T(8,128)S(1)}, u32[]{:S(2)}, u32[]{:S(2)}) collective-permute-start(f32[32,128,128]{2,1,0:T(8,128)S(1)} %get-tuple-element.12), channel_id=1, source_target_pairs={{0,1},{1,0},{2,3},{3,2},{4,5},{5,4},{6,7},{7,6},{8,9},{9,8},{10,11... | collective-permute-start | bytes 6291464 | tf_op jit(solution)/shard_map/ppermute | solution.py:199
  80.8 4.4 %collective-permute-start.1 = (f32[32,128,128]{2,1,0:T(8,128)S(1)}, f32[32,128,128]{2,1,0:T(8,128)S(1)}, u32[]{:S(2)}, u32[]{:S(2)}) collective-permute-start(f32[32,128,128]{2,1,0:T(8,128)S(1)} %half_terms.7), channel_id=1, source_target_pairs={{0,1},{1,0},{2,3},{3,2},{4,5},{5,4},{6,7},{7,6},{8,9},{9,8},{10,11... | collective-permute-start | bytes 6291464 | tf_op jit(solution)/shard_map/ppermute | solution.py:199
  85.8 21.2 %copy-start.2 = (bf16[512,128]{1,0:T(8,128)(2,1)S(1)}, bf16[512,128]{1,0:T(8,128)(2,1)}, u32[]{:S(2)}) copy-start(bf16[512,128]{1,0:T(8,128)(2,1)} %param.4) | copy-start | bytes 393220
  127.9 4.2 %collective-permute-start.2 = (f32[32,128,128]{2,1,0:T(8,128)S(1)}, f32[32,128,128]{2,1,0:T(8,128)S(1)}, u32[]{:S(2)}, u32[]{:S(2)}) collective-permute-start(f32[32,128,128]{2,1,0:T(8,128)S(1)} %half_terms.9), channel_id=1, source_target_pairs={{0,1},{1,0},{2,3},{3,2},{4,5},{5,4},{6,7},{7,6},{8,9},{9,8},{10,11... | collective-permute-start | bytes 6291464 | tf_op jit(solution)/shard_map/ppermute | solution.py:199
where the time goes:
time: 158 us; the launch traced here: 155 us
  blocking collectives  102 us (65%)
  Pallas kernels  19 us (12%)
  waiting for transfers between devices  16.3 us (10%)
  starting transfers between devices  12.6 us (8%)
  other arithmetic  2.51 us (2%)
  local copies, waits for them, and re-layouts  2.34 us (1%)
    all_to_all x3, blocking collectives, multiply(): parts = lax.all_to_all(scaled, 'col', 0, 0, axis_index_groups=alike)  62.8 us
    all_to_all x2, blocking collectives, multiply(): gathered = lax.all_to_all(spread, 'row', 0, 0).reshape(-1, size, width)  38.9 us
    all_to_all x1, waiting for transfers between devices, multiply(): gathered = lax.all_to_all(spread, 'row', 0, 0).reshape(-1, size, width)  10.5 us
    pallas_call x5, Pallas kernels, half_terms(): pl.pallas_call(functools.partial(half_kernel, half=half), in_specs=[smem,...  9.74 us
    all_to_all x1, starting transfers between devices, multiply(): gathered = lax.all_to_all(spread, 'row', 0, 0).reshape(-1, size, width)  8.09 us
    ppermute x3, waiting for transfers between devices, multiply(): taken = lax.ppermute(given, 'col', swap)  5.79 us
    ppermute x3, starting transfers between devices, multiply(): taken = lax.ppermute(given, 'col', swap)  4.47 us
    pallas_call x1, Pallas kernels, make_lists(): pl.pallas_call(functools.partial(pair_list, groups=groups, height=height)...  3.97 us
  transfers between devices with their start and end apart: 4, of which 4 were waited for; matrix products, arithmetic and copies ran while one was open for 0% of the time, Pallas kernels for 6%

commit v1 on v0

v1 whole, which is shorter than its diff:
```python
import functools

import jax
import jax.numpy as jnp
from jax import lax
from jax.experimental import pallas as pl
from jax.experimental.pallas import tpu as pltpu
from jax.sharding import PartitionSpec as P

UNROLL = 24
PART = 16
MOST = 12
LISTS = 4
MIB = 1024 * 1024


def pair_list(core_ref, order_ref, pointer_ref, column_ref, after_ref, word_ref, count_ref, *, height):
    del after_ref
    core = core_ref[0]
    rows = pointer_ref.shape[0] - 1
    slots = rows // height // 2
    part = slots // 2

    for index in range(LISTS):
        late, own = index // 2, index % 2
        which = core if own else 1 - core

        def one_row(local, number):
            row = (2 * order_ref[late * part + local // height] + which) * height + local % height
            first, last = pointer_ref[row], pointer_ref[row + 1]

            def one_pair(k, _):
                j = first + 2 * k
                both = (j + 1 < last).astype(jnp.int32)
                word_ref[index, number + k] = (
                    j + local * 512 + column_ref[j] * 16384 + column_ref[j + both] * 524288 + (1 + both) * 16777216
                )
                return 0

            pairs = (last - first + 1) // 2
            lax.fori_loop(0, pairs, one_pair, 0)
            return number + pairs

        total = lax.fori_loop(0, part * height, one_row, 0)
        last = word_ref[index, total - 1] & 16383
        for k in range(UNROLL):
            word_ref[index, total + k] = last
        count_ref[index] = (total + UNROLL - 1) // UNROLL


def make_lists(core, order, pointer, columns, after, height):
    rows = pointer.shape[0] - 1
    smem = pl.BlockSpec(memory_space=pltpu.SMEM)
    width = (rows // LISTS) * (MOST // 2) + UNROLL
    return pl.pallas_call(
        functools.partial(pair_list, height=height),
        in_specs=[smem] * 4 + [pl.BlockSpec(memory_space=pl.ANY)],
        out_specs=[smem] * 2,
        out_shape=[
            jax.ShapeDtypeStruct((LISTS, width), jnp.int32),
            jax.ShapeDtypeStruct((LISTS,), jnp.int32),
        ],
        compiler_params=pltpu.CompilerParams(vmem_limit_bytes=2 * MIB),
        name="pair_list",
    )(core, order, pointer, columns, after)


def add_pairs(word_ref, count_ref, vector_ref, block_ref, out_ref, index, height, ready, arrive):
    out_ref[...] = jnp.zeros_like(out_ref)

    def body(step, ready):
        ready = arrive((word_ref[index, step * UNROLL + UNROLL - 1] >> 9 & 31) // height + 1, ready)
        for k in range(UNROLL):
            word = word_ref[index, step * UNROLL + k]
            j = word & 511
            row = (word >> 9) & 31
            c1 = (word >> 14) & 31
            c2 = (word >> 19) & 31
            n = word >> 24
            left = jnp.concatenate([block_ref[j], block_ref[j + (n >> 1)]], axis=1)
            v1 = vector_ref[c1]
            v2 = vector_ref[c2]
            right = jnp.concatenate([jnp.where(n > 0, v1, jnp.zeros_like(v1)), jnp.where(n > 1, v2, jnp.zeros_like(v2))], axis=0)
            out_ref[row] += jnp.dot(left, right, preferred_element_type=jnp.float32)
        return ready

    return lax.fori_loop(0, count_ref[index], body, ready)


def first_kernel(order_ref, pointer_ref, word_ref, count_ref, vector_ref, source_ref, out_ref, block_ref, sem, *, height):
    capacity = source_ref.shape[0]
    slots = order_ref.shape[0]

    def span(slot):
        row = 2 * order_ref[slot] * height
        first, last = pointer_ref[row], pointer_ref[row + 2 * height]
        return first, (last - first + PART - 1) // PART

    def copy(slot, first, k):
        part = pl.ds(jnp.minimum(first + k * PART, capacity - PART), PART)
        return pltpu.make_async_copy(source_ref.at[part], block_ref.at[part], sem.at[slot, k])

    def start(slot, _):
        first, parts = span(slot)

        def one(k, _):
            copy(slot, first, k).start()
            return 0

        return lax.fori_loop(0, parts, one, 0)

    def wait(slot, _):
        first, parts = span(slot)

        def one(k, _):
            copy(slot, first, k).wait()
            return 0

        return lax.fori_loop(0, parts, one, 0)

    def arrive(needed, ready):
        lax.fori_loop(ready, needed, wait, 0)
        return needed

    lax.fori_loop(0, slots, start, 0)
    ready = add_pairs(word_ref, count_ref, vector_ref, block_ref, out_ref, 0, height, 0, arrive)
    lax.fori_loop(ready, slots, wait, 0)


def some_kernel(word_ref, count_ref, vector_ref, block_ref, out_ref, *, index, height):
    add_pairs(word_ref, count_ref, vector_ref, block_ref, out_ref, index, height, 0, lambda needed, ready: ready)


def first_terms(order, pointer, words, counts, vector, tile_blocks, height):
    smem = pl.BlockSpec(memory_space=pltpu.SMEM)
    vmem = pl.BlockSpec(memory_space=pltpu.VMEM)
    rows = (pointer.shape[0] - 1) // LISTS
    return pl.pallas_call(
        functools.partial(first_kernel, height=height),
        in_specs=[smem] * 4 + [vmem, pl.BlockSpec(memory_space=pl.ANY)],
        out_specs=[vmem, vmem],
        out_shape=[
            jax.ShapeDtypeStruct((rows, tile_blocks.shape[1], vector.shape[2]), jnp.float32),
            pltpu.VMEM(tile_blocks.shape, tile_blocks.dtype),
        ],
        scratch_shapes=[pltpu.SemaphoreType.DMA((order.shape[0], 2 * height * MOST // PART))],
        compiler_params=pltpu.CompilerParams(vmem_limit_bytes=24 * MIB),
        name="first_terms",
    )(order, pointer, words, counts, vector, pltpu.with_memory_space_constraint(tile_blocks, pltpu.HBM))


def some_terms(words, counts, vector, held, index, rows, height):
    smem = pl.BlockSpec(memory_space=pltpu.SMEM)
    vmem = pl.BlockSpec(memory_space=pltpu.VMEM)
    size = held.shape[1]
    return pl.pallas_call(
        functools.partial(some_kernel, index=index, height=height),
        in_specs=[smem, smem, vmem, vmem],
        out_specs=vmem,
        out_shape=jax.ShapeDtypeStruct((rows, size, vector.shape[2]), jnp.float32),
        compiler_params=pltpu.CompilerParams(vmem_limit_bytes=24 * MIB),
        cost_estimate=pl.CostEstimate(
            flops=2 * rows * 8 * size**3, bytes_accessed=rows * 8 * size * size, transcendentals=0
        ),
        name="some_terms",
    )(words, counts, vector, pltpu.with_memory_space_constraint(held, pltpu.VMEM))


def combine_kernel(*refs):
    *terms, out_ref = refs
    chips, taller, width = out_ref.shape
    rows, size, _ = terms[0].shape
    height = rows // chips
    step = 32
    tops = []
    for chip in range(chips):
        most = jnp.zeros((step, width), jnp.float32)
        for k in range(height):
            row = chip * height + k
            for t in range(0, size, step):
                both = terms[0][row, t : t + step]
                for term in terms[1:]:
                    both = both + term[row, t : t + step]
                out_ref[chip, k * size + t : k * size + t + step] = both
                most = jnp.maximum(most, jnp.abs(both))
        tops.append(jnp.max(most, axis=0, keepdims=True))
    most = jnp.max(jnp.concatenate(tops, axis=0), axis=1, keepdims=True)
    power = jnp.floor(jnp.log2(jnp.maximum(most, 1e-30))) - 14.0
    power = jnp.broadcast_to(power, (chips, width))
    scale = jnp.exp2(-power)
    for chip in range(chips):
        by = jnp.broadcast_to(scale[chip : chip + 1], (step, width))
        for t in range(0, height * size, step):
            out_ref[chip, t : t + step] = out_ref[chip, t : t + step] * by
        out_ref[chip, height * size :] = jnp.broadcast_to(power[chip : chip + 1], (taller - height * size, width))


def combine(chips, *terms):
    vmem = pl.BlockSpec(memory_space=pltpu.VMEM)
    rows, size, width = terms[0].shape
    return pl.pallas_call(
        combine_kernel,
        in_specs=[vmem] * len(terms),
        out_specs=vmem,
        out_shape=jax.ShapeDtypeStruct((chips, rows // chips * size + 8, width), jnp.float32),
        compiler_params=pltpu.CompilerParams(vmem_limit_bytes=24 * MIB),
        name="combine",
    )(*terms)


def per_device(subspace, blocks, row_pointer, block_column):
    tile_blocks = blocks[0, 0]
    pointer = row_pointer[0, 0]
    size = tile_blocks.shape[1]
    own_rows, width = subspace.shape
    height = own_rows // size
    chips = lax.axis_size("col") // 2
    core = lax.axis_index("col") % 2
    swap = [(c, c ^ 1) for c in range(2 * chips)]
    ring = lax.axis_size("row") // 2
    here = lax.axis_index("row")
    loop = chips // 2
    chip = lax.axis_index("col") // 2

    source = block_column[0, 0] // height
    apart = (source - here) % ring
    same = jnp.where(apart == 0, 0, jnp.where(apart == 1, 3, jnp.where(apart == 2, 6, 2)))
    other = jnp.where(apart == 0, 1, jnp.where(apart == 1, 5, jnp.where(apart == 2, 7, 4)))
    slot = jnp.where(source // ring == here // ring, same, other)
    place = (slot * height + block_column[0, 0] % height).astype(jnp.int32)

    k = jnp.arange(chips, dtype=jnp.int32)
    away_z = ((k == 0) | (k == 1) | (k == 3) | (k == 5)).astype(jnp.int32)
    away_y = jnp.where((k == 0) | (k == 6), 1, jnp.where((k == 1) | (k == 7), 3, jnp.where((k == 2) | (k == 3), 2, 0)))
    order = (chip // loop + away_z) % 2 * loop + (chip + away_y) % loop
    order = order.astype(jnp.int32)

    def shift(x, dz, dx):
        pairs = [(z * ring + k, (z + dz) % 2 * ring + (k + dx) % ring) for z in range(2) for k in range(ring)]
        return lax.ppermute(x, "row", pairs)

    def pass_on(x, dz, dy):
        pairs = []
        for z in range(2):
            for y in range(loop):
                for c in range(2):
                    to = (z + dz) % 2 * loop + (y + dy) % loop
                    pairs.append(((z * loop + y) * 2 + c, to * 2 + c))
        return lax.ppermute(x, "col", pairs)

    def gather(vector):
        below, above, across = shift(vector, 0, 1), shift(vector, 0, -1), shift(vector, 1, 0)
        near = jnp.concatenate([vector, across])
        sides = jnp.concatenate([below, above])
        opposite = shift(near, 0, 2)
        far = shift(sides, 1, 0)
        return jnp.concatenate([near, sides, far, opposite]).reshape(-1, size, width), sides

    def widened(x):
        weight = jnp.exp2(x[:, own_rows : own_rows + 1].astype(jnp.float32))
        return x[:, :own_rows].astype(jnp.float32) * weight

    def multiply(vector, lists, held):
        gathered, sides = gather(vector)
        if lists is None:
            lists = make_lists(core.reshape(1), order, pointer, place, sides, height)
        words, counts = lists
        rows = loop * height
        if held is None:
            given, held = first_terms(order, pointer, words, counts, gathered, tile_blocks, height)
        else:
            given = some_terms(words, counts, gathered, held, 0, rows, height)
        taken = lax.ppermute(given, "col", swap)
        kept = some_terms(words, counts, gathered, held, 1, rows, height)
        early = combine(loop, kept, taken).astype(jnp.float16)
        across = pass_on(early[:2], 1, 0)
        opposite = pass_on(early[2:], 0, 2)
        given = some_terms(words, counts, gathered, held, 2, rows, height)
        taken = lax.ppermute(given, "col", swap)
        kept = some_terms(words, counts, gathered, held, 3, rows, height)
        passed = jnp.concatenate([widened(opposite), widened(across)]).reshape(kept.shape)
        late = combine(loop, kept, taken, passed)
        half = late.astype(jnp.float16)
        parts = [pass_on(half[1:2], 1, 0), pass_on(half[2:3], 0, 1), pass_on(half[3:4], 0, -1)]
        total = widened(late[:1])
        for part in parts:
            total = total + widened(part)
        return total[0], lists, held

    total, lists, held = multiply(subspace, None, None)
    first = total.astype(jnp.bfloat16)
    total, lists, held = multiply(first, lists, held)
    second = (2.0 * total - subspace.astype(jnp.float32)).astype(jnp.bfloat16)
    total, lists, held = multiply(second, lists, held)
    return 2.0 * total - first.astype(jnp.float32)


def solution(mesh):
    placed = (
        P(("row", "col"), None),
        P("row", "col", None, None, None),
        P("row", "col", None),
        P("row", "col", None),
    )
    return jax.shard_map(
        per_device, mesh=mesh, in_specs=placed, out_specs=P(("row", "col"), None), check_vma=False
    )
```

time: 158 us -> 146 us (0.924); the launches traced: 155 us -> 145 us
  blocking collectives: 102 us -> 0 us
  waiting for transfers between devices: 16.3 us -> 70.4 us
  starting transfers between devices: 12.6 us -> 45.7 us
  Pallas kernels: 19 us -> 23.7 us
    all_to_all x5 -> x0, blocking collectives: 102 us -> none  [the longest x3 62.8 us: multiply(): parts = lax.all_to_all(scaled, 'col', 0, 0, axis_index_groups=alike)]
    ppermute x0 -> x30, waiting for transfers between devices: none -> 66.4 us  [the longest x15 34.2 us: pass_on(): return lax.ppermute(x, 'col', pairs)]
    ppermute x0 -> x30, starting transfers between devices: none -> 45.2 us  [the longest x15 24.8 us: shift(): return lax.ppermute(x, 'row', pairs)]
    all_to_all x1 -> x0, waiting for transfers between devices: 10.5 us -> none  [multiply(): gathered = lax.all_to_all(spread, 'row', 0, 0).reshape(-1, size, width)]
    all_to_all x1 -> x0, starting transfers between devices: 8.09 us -> none  [multiply(): gathered = lax.all_to_all(spread, 'row', 0, 0).reshape(-1, size, width)]
    pallas_call x10 -> x19, Pallas kernels: 19 us -> 23.7 us  [the longest x11 14.2 us: some_terms(): pl.pallas_call(functools.partial(some_kernel, index=index, height=height)...]
    ppermute x3 -> x6, starting transfers between devices: 4.47 us -> 0.51 us  [multiply(): taken = lax.ppermute(given, 'col', swap)]
    broadcast_in_dim x3 -> x0, local copies, waits for them, and re-layouts: 2.33 us -> none  [multiply(): spread = jnp.broadcast_to(vector[None], (sources, own_rows, width))]
  transfers between devices with their start and end apart: 4 -> 36, of which waited for: 4 -> 28; matrix products, arithmetic and copies ran while one was open for 0% -> 1% of each run, Pallas kernels for 6% -> 11%
where the time goes in v1:
time: 146 us; the launch traced here: 145 us
  waiting for transfers between devices  70.4 us (48%)
  starting transfers between devices  45.7 us (31%)
  Pallas kernels  23.7 us (16%)
  other arithmetic  2.19 us (2%)
  local copies, waits for them, and re-layouts  1.94 us (1%)
    ppermute x15, waiting for transfers between devices, pass_on(): return lax.ppermute(x, 'col', pairs)  34.2 us
    ppermute x15, waiting for transfers between devices, shift(): return lax.ppermute(x, 'row', pairs)  32.2 us
    ppermute x15, starting transfers between devices, shift(): return lax.ppermute(x, 'row', pairs)  24.8 us
    ppermute x15, starting transfers between devices, pass_on(): return lax.ppermute(x, 'col', pairs)  20.4 us
    pallas_call x11, Pallas kernels, some_terms(): pl.pallas_call(functools.partial(some_kernel, index=index, height=height)...  14.2 us
    pallas_call x1, Pallas kernels, make_lists(): pl.pallas_call(functools.partial(pair_list, height=height), in_specs=[sme...  4.25 us
    ppermute x6, waiting for transfers between devices, multiply(): taken = lax.ppermute(given, 'col', swap)  3.93 us
    pallas_call x1, Pallas kernels, first_terms(): pl.pallas_call(functools.partial(first_kernel, height=height), in_specs=[...  3.3 us
  transfers between devices with their start and end apart: 36, of which 28 were waited for; matrix products, arithmetic and copies ran while one was open for 1% of the time, Pallas kernels for 11%

profile of v1, /device:TPU:6, one launch (start us, length us, event | category | flops | bytes accessed | tf_op | source)
XLA Modules:
  0.0 144.6 jit_solution(17280489061586163722)
XLA Ops:
  0.0 4.0 %collective-permute-start.2 = (bf16[512,128]{1,0:T(8,128)(2,1)}, bf16[512,128]{1,0:T(8,128)(2,1)S(1)}, u32[]{:S(2)}, u32[]{:S(2)}) collective-permute-start(bf16[512,128]{1,0:T(8,128)(2,1)} %param.4), channel_id=1, source_target_pairs={{0,64},{16,80},{32,96},{48,112},{64,0},{80,16},{96,32},{112,48},{1... | collective-permute-start | bytes 393224 | tf_op jit(solution)/shard_map/ppermute | solution.py:240
  4.0 0.5 collective-permute-start
  4.4 1.5 %collective-permute-start.1 = (bf16[512,128]{1,0:T(8,128)(2,1)}, bf16[512,128]{1,0:T(8,128)(2,1)S(1)}, u32[]{:S(2)}, u32[]{:S(2)}) collective-permute-start(bf16[512,128]{1,0:T(8,128)(2,1)} %param.4), channel_id=1, source_target_pairs={{0,48},{16,0},{32,16},{48,32},{64,112},{80,64},{96,80},{112,96},{1... | collective-permute-start | bytes 393224 | tf_op jit(solution)/shard_map/ppermute | solution.py:240
  6.0 0.9 constant_dynamic-update-slice_fusion.7
  7.0 0.7 collective-permute-done.2
  7.7 1.4 %collective-permute-done = bf16[512,128]{1,0:T(8,128)(2,1)S(1)} collective-permute-done((bf16[512,128]{1,0:T(8,128)(2,1)}, bf16[512,128]{1,0:T(8,128)(2,1)S(1)}, u32[]{:S(2)}, u32[]{:S(2)}) %collective-permute-start) | collective-permute-done | bytes 131104 | tf_op jit(solution)/shard_map/ppermute | solution.py:240
  9.2 1.7 %collective-permute-done.1 = bf16[512,128]{1,0:T(8,128)(2,1)S(1)} collective-permute-done((bf16[512,128]{1,0:T(8,128)(2,1)}, bf16[512,128]{1,0:T(8,128)(2,1)S(1)}, u32[]{:S(2)}, u32[]{:S(2)}) %collective-permute-start.1) | collective-permute-done | bytes 131104 | tf_op jit(solution)/shard_map/ppermute | solution.py:240
  11.1 1.5 %collective-permute-start.4 = (bf16[1024,128]{1,0:T(8,128)(2,1)S(1)}, bf16[1024,128]{1,0:T(8,128)(2,1)S(1)}, u32[]{:S(2)}, u32[]{:S(2)}) collective-permute-start(bf16[1024,128]{1,0:T(8,128)(2,1)S(1)} %pad_maximum_fusion.3), channel_id=1, source_target_pairs={{0,32},{16,48},{32,0},{48,16},{64,96},{80,112},{96,64},{112,80},{1... | collective-permute-start | bytes 786440 | tf_op jit(solution)/shard_map/ppermute | solution.py:240
  12.7 4.2 %pair_list.1 = (s32[4,120]{1,0:T(4,128)S(1)}, s32[4]{0:T(128)S(1)}) custom-call(s32[1]{0:T(128)} %bitcast.core_ref, s32[8]{0:T(128)S(1)} %fusion.38.order_ref, s32[65]{0:T(128)S(1)} %bitcast.69, s32[512]{0:T(512)S(1)} %fusion.21.column_ref, bf16[1024,128]{1,0:T(8,128)(2,1)S(1)} %get-tuple-element.33.after_ref), custom_call_target="tpu_custom_call" | custom-call | tf_op jit(solution)/shard_map/pair_list/pallas_call | solution.py:55
  17.0 1.8 %collective-permute-done.3 = bf16[1024,128]{1,0:T(8,128)(2,1)S(1)} collective-permute-done((bf16[1024,128]{1,0:T(8,128)(2,1)S(1)}, bf16[1024,128]{1,0:T(8,128)(2,1)S(1)}, u32[]{:S(2)}, u32[]{:S(2)}) %collective-permute-start.3) | collective-permute-done | bytes 262176 | tf_op jit(solution)/shard_map/ppermute | solution.py:240
  18.9 0.8 collective-permute-done.4
  19.7 3.3 %first_terms.1 = (f32[16,128,128]{2,1,0:T(8,128)S(1)}, bf16[512,128,128]{2,1,0:T(8,128)(2,1)S(1)}) custom-call(s32[8]{0:T(128)S(1)} %fusion.38.order_ref, s32[65]{0:T(128)S(1)} %bitcast.70, s32[4,120]{1,0:T(4,128)S(1)} %get-tuple-element.9.word_ref, s32[4]{0:T(128)S(1)} %get-tuple-element.10.count_ref, bf16[32,128,128]{2,1,0:T(8,128)(2,1)S(1)} %bitcast.62, ...), custom_call_target="tpu_custom_call" | custom-call | tf_op jit(solution)/shard_map/first_terms/pallas_call | solution.py:138
  23.1 1.3 some_terms.13.refs_0_
  24.3 1.4 collective-permute-done.6.refs_1_
  26.2 3.3 %collective-permute-start.7 = (f16[2,520,128]{2,1,0:T(8,128)(2,1)S(1)}, f16[2,520,128]{2,1,0:T(8,128)(2,1)S(1)}, u32[]{:S(2)}, u32[]{:S(2)}) collective-permute-start(f16[2,520,128]{2,1,0:T(8,128)(2,1)S(1)} %get-tuple-element.30), channel_id=1, source_target_pairs={{0,4},{1,5},{2,6},{3,7},{4,0},{5,1},{6,2},{7,3},{8,12},{9,13},{10,... | collective-permute-start | bytes 798728 | tf_op jit(solution)/shard_map/ppermute | solution.py:249
  29.5 1.3 some_terms.12
  30.9 1.1 collective-permute-start.8
  32.0 1.3 some_terms.11.refs_0_
  33.3 3.0 %collective-permute-done.7 = f16[2,520,128]{2,1,0:T(8,128)(2,1)S(1)} collective-permute-done((f16[2,520,128]{2,1,0:T(8,128)(2,1)S(1)}, f16[2,520,128]{2,1,0:T(8,128)(2,1)S(1)}, u32[]{:S(2)}, u32[]{:S(2)}) %collective-permute-start.7) | collective-permute-done | bytes 266272 | tf_op jit(solution)/shard_map/ppermute | solution.py:249
  36.3 3.4 %collective-permute-done.8 = f16[2,520,128]{2,1,0:T(8,128)(2,1)S(1)} collective-permute-done((f16[2,520,128]{2,1,0:T(8,128)(2,1)S(1)}, f16[2,520,128]{2,1,0:T(8,128)(2,1)S(1)}, u32[]{:S(2)}, u32[]{:S(2)}) %collective-permute-start.8) | collective-permute-done | bytes 266272 | tf_op jit(solution)/shard_map/ppermute | solution.py:249
  40.4 1.1 collective-permute-start.11
  41.5 1.0 collective-permute-start.10
  42.5 1.0 collective-permute-start.9
  43.5 2.0 %collective-permute-done.11 = f16[1,520,128]{2,1,0:T(8,128)(2,1)S(1)} collective-permute-done((f16[1,520,128]{2,1,0:T(8,128)(2,1)S(1)}, f16[1,520,128]{2,1,0:T(8,128)(2,1)S(1)}, u32[]{:S(2)}, u32[]{:S(2)}) %collective-permute-start.11) | collective-permute-done | bytes 133152 | tf_op jit(solution)/shard_map/ppermute | solution.py:249
  45.6 2.2 %collective-permute-done.10 = f16[1,520,128]{2,1,0:T(8,128)(2,1)S(1)} collective-permute-done((f16[1,520,128]{2,1,0:T(8,128)(2,1)S(1)}, f16[1,520,128]{2,1,0:T(8,128)(2,1)S(1)}, u32[]{:S(2)}, u32[]{:S(2)}) %collective-permute-start.10) | collective-permute-done | bytes 133152 | tf_op jit(solution)/shard_map/ppermute | solution.py:249
  47.9 6.4 %collective-permute-start.12 = (bf16[512,128]{1,0:T(8,128)(2,1)S(1)}, bf16[512,128]{1,0:T(8,128)(2,1)S(1)}, u32[]{:S(2)}, u32[]{:S(2)}) collective-permute-start(bf16[512,128]{1,0:T(8,128)(2,1)S(1)} %get-tuple-element.16), channel_id=1, source_target_pairs={{0,64},{16,80},{32,96},{48,112},{64,0},{80,16},{96,32},{112,48},{1... | collective-permute-start | bytes 393224 | tf_op jit(solution)/shard_map/ppermute | solution.py:240
  54.3 2.0 %collective-permute-start.14 = (bf16[512,128]{1,0:T(8,128)(2,1)S(1)}, bf16[512,128]{1,0:T(8,128)(2,1)S(1)}, u32[]{:S(2)}, u32[]{:S(2)}) collective-permute-start(bf16[512,128]{1,0:T(8,128)(2,1)S(1)} %get-tuple-element.16), channel_id=1, source_target_pairs={{0,48},{16,0},{32,16},{48,32},{64,112},{80,64},{96,80},{112,96},{1... | collective-permute-start | bytes 393224 | tf_op jit(solution)/shard_map/ppermute | solution.py:240
  56.3 0.9 collective-permute-done.12
  57.4 3.3 %collective-permute-done.13 = bf16[512,128]{1,0:T(8,128)(2,1)S(1)} collective-permute-done((bf16[512,128]{1,0:T(8,128)(2,1)S(1)}, bf16[512,128]{1,0:T(8,128)(2,1)S(1)}, u32[]{:S(2)}, u32[]{:S(2)}) %collective-permute-start.13) | collective-permute-done | bytes 131104 | tf_op jit(solution)/shard_map/ppermute | solution.py:240
  60.7 5.3 %collective-permute-done.14 = bf16[512,128]{1,0:T(8,128)(2,1)S(1)} collective-permute-done((bf16[512,128]{1,0:T(8,128)(2,1)S(1)}, bf16[512,128]{1,0:T(8,128)(2,1)S(1)}, u32[]{:S(2)}, u32[]{:S(2)}) %collective-permute-start.14) | collective-permute-done | bytes 131104 | tf_op jit(solution)/shard_map/ppermute | solution.py:240
  66.2 7.8 %collective-permute-done.15 = bf16[1024,128]{1,0:T(8,128)(2,1)S(1)} collective-permute-done((bf16[1024,128]{1,0:T(8,128)(2,1)S(1)}, bf16[1024,128]{1,0:T(8,128)(2,1)S(1)}, u32[]{:S(2)}, u32[]{:S(2)}) %collective-permute-start.15) | collective-permute-done | bytes 262176 | tf_op jit(solution)/shard_map/ppermute | solution.py:240
  74.1 1.3 some_terms.17
  75.4 1.5 %some_terms.16.refs_0_ = f32[16,128,128]{2,1,0:T(8,128)S(1)} custom-call(s32[4,120]{1,0:T(4,128)S(1)} %get-tuple-element.9.word_ref, s32[4]{0:T(128)S(1)} %get-tuple-element.10.count_ref, bf16[32,128,128]{2,1,0:T(8,128)(2,1)S(1)} %bitcast.55, bf16[512,128,128]{2,1,0:T(8,128)(2,1)S(1)} %get-tuple-element.11.block_ref), custom_call_target="tpu_custom_call" | custom-call | flops 536870912 | bytes 2097152 | tf_op jit(solution)/shard_map/some_terms/pallas_call | solution.py:156
  76.9 1.2 collective-permute-done.18.refs_1_
  78.6 0.6 collective-permute-start.19
  79.2 1.3 some_terms.15
  80.6 1.0 collective-permute-start.20
  81.6 1.3 some_terms.14.refs_0_
  82.9 5.7 %collective-permute-done.19 = f16[2,520,128]{2,1,0:T(8,128)(2,1)S(1)} collective-permute-done((f16[2,520,128]{2,1,0:T(8,128)(2,1)S(1)}, f16[2,520,128]{2,1,0:T(8,128)(2,1)S(1)}, u32[]{:S(2)}, u32[]{:S(2)}) %collective-permute-start.19) | collective-permute-done | bytes 266272 | tf_op jit(solution)/shard_map/ppermute | solution.py:249
  88.6 0.8 collective-permute-done.20
  90.1 2.7 %collective-permute-start.23 = (f16[1,520,128]{2,1,0:T(8,128)(2,1)S(1)}, f16[1,520,128]{2,1,0:T(8,128)(2,1)S(1)}, u32[]{:S(2)}, u32[]{:S(2)}) collective-permute-start(f16[1,520,128]{2,1,0:T(8,128)(2,1)S(1)} %get-tuple-element.23), channel_id=1, source_target_pairs={{0,6},{1,7},{2,0},{3,1},{4,2},{5,3},{6,4},{7,5},{8,14},{9,15},{10,... | collective-permute-start | bytes 399368 | tf_op jit(solution)/shard_map/ppermute | solution.py:249
  92.8 0.9 collective-permute-start.21
  93.6 2.3 %collective-permute-done.23 = f16[1,520,128]{2,1,0:T(8,128)(2,1)S(1)} collective-permute-done((f16[1,520,128]{2,1,0:T(8,128)(2,1)S(1)}, f16[1,520,128]{2,1,0:T(8,128)(2,1)S(1)}, u32[]{:S(2)}, u32[]{:S(2)}) %collective-permute-start.23) | collective-permute-done | bytes 133152 | tf_op jit(solution)/shard_map/ppermute | solution.py:249
  95.9 3.0 %collective-permute-done.22 = f16[1,520,128]{2,1,0:T(8,128)(2,1)S(1)} collective-permute-done((f16[1,520,128]{2,1,0:T(8,128)(2,1)S(1)}, f16[1,520,128]{2,1,0:T(8,128)(2,1)S(1)}, u32[]{:S(2)}, u32[]{:S(2)}) %collective-permute-start.22) | collective-permute-done | bytes 133152 | tf_op jit(solution)/shard_map/ppermute | solution.py:249
  99.1 1.4 collective-permute-start.24
  100.5 2.0 %collective-permute-start.26 = (bf16[512,128]{1,0:T(8,128)(2,1)S(1)}, bf16[512,128]{1,0:T(8,128)(2,1)S(1)}, u32[]{:S(2)}, u32[]{:S(2)}) collective-permute-start(bf16[512,128]{1,0:T(8,128)(2,1)S(1)} %get-tuple-element.14), channel_id=1, source_target_pairs={{0,48},{16,0},{32,16},{48,32},{64,112},{80,64},{96,80},{112,96},{1... | collective-permute-start | bytes 393224 | tf_op jit(solution)/shard_map/ppermute | solution.py:240
  102.6 3.1 %collective-permute-done.24 = bf16[512,128]{1,0:T(8,128)(2,1)S(1)} collective-permute-done((bf16[512,128]{1,0:T(8,128)(2,1)S(1)}, bf16[512,128]{1,0:T(8,128)(2,1)S(1)}, u32[]{:S(2)}, u32[]{:S(2)}) %collective-permute-start.24) | collective-permute-done | bytes 131104 | tf_op jit(solution)/shard_map/ppermute | solution.py:240
  105.8 1.1 collective-permute-done.25
  106.9 4.9 %collective-permute-start.27 = (bf16[1024,128]{1,0:T(8,128)(2,1)S(1)}, bf16[1024,128]{1,0:T(8,128)(2,1)S(1)}, u32[]{:S(2)}, u32[]{:S(2)}) collective-permute-start(bf16[1024,128]{1,0:T(8,128)(2,1)S(1)} %pad_maximum_fusion.6), channel_id=1, source_target_pairs={{0,64},{16,80},{32,96},{48,112},{64,0},{80,16},{96,32},{112,48},{1... | collective-permute-start | bytes 786440 | tf_op jit(solution)/shard_map/ppermute | solution.py:240
  111.9 4.3 %collective-permute-done.27 = bf16[1024,128]{1,0:T(8,128)(2,1)S(1)} collective-permute-done((bf16[1024,128]{1,0:T(8,128)(2,1)S(1)}, bf16[1024,128]{1,0:T(8,128)(2,1)S(1)}, u32[]{:S(2)}, u32[]{:S(2)}) %collective-permute-start.27) | collective-permute-done | bytes 262176 | tf_op jit(solution)/shard_map/ppermute | solution.py:240
  116.3 1.3 some_terms.21
  117.6 1.3 some_terms.20.refs_0_
  118.9 1.4 collective-permute-done.30.refs_1_
  120.8 5.0 %collective-permute-start.31 = (f16[2,520,128]{2,1,0:T(8,128)(2,1)S(1)}, f16[2,520,128]{2,1,0:T(8,128)(2,1)S(1)}, u32[]{:S(2)}, u32[]{:S(2)}) collective-permute-start(f16[2,520,128]{2,1,0:T(8,128)(2,1)S(1)} %get-tuple-element.20), channel_id=1, source_target_pairs={{0,4},{1,5},{2,6},{3,7},{4,0},{5,1},{6,2},{7,3},{8,12},{9,13},{10,... | collective-permute-start | bytes 798728 | tf_op jit(solution)/shard_map/ppermute | solution.py:249
  125.8 1.3 some_terms.19
  127.1 0.4 collective-permute-start.32
  127.5 1.3 some_terms.18.refs_0_
  128.8 3.6 %collective-permute-done.31 = f16[2,520,128]{2,1,0:T(8,128)(2,1)S(1)} collective-permute-done((f16[2,520,128]{2,1,0:T(8,128)(2,1)S(1)}, f16[2,520,128]{2,1,0:T(8,128)(2,1)S(1)}, u32[]{:S(2)}, u32[]{:S(2)}) %collective-permute-start.31) | collective-permute-done | bytes 266272 | tf_op jit(solution)/shard_map/ppermute | solution.py:249
  132.5 3.5 %collective-permute-done.32 = f16[2,520,128]{2,1,0:T(8,128)(2,1)S(1)} collective-permute-done((f16[2,520,128]{2,1,0:T(8,128)(2,1)S(1)}, f16[2,520,128]{2,1,0:T(8,128)(2,1)S(1)}, u32[]{:S(2)}, u32[]{:S(2)}) %collective-permute-start.32) | collective-permute-done | bytes 266272 | tf_op jit(solution)/shard_map/ppermute | solution.py:249
  136.7 2.0 %collective-permute-start.34 = (f16[1,520,128]{2,1,0:T(8,128)(2,1)S(1)}, f16[1,520,128]{2,1,0:T(8,128)(2,1)S(1)}, u32[]{:S(2)}, u32[]{:S(2)}) collective-permute-start(f16[1,520,128]{2,1,0:T(8,128)(2,1)S(1)} %get-tuple-element.19), channel_id=1, source_target_pairs={{0,2},{1,3},{2,4},{3,5},{4,6},{5,7},{6,0},{7,1},{8,10},{9,11},{10,... | collective-permute-start | bytes 399368 | tf_op jit(solution)/shard_map/ppermute | solution.py:249
  139.1 2.7 %collective-permute-done.35 = f16[1,520,128]{2,1,0:T(8,128)(2,1)S(1)} collective-permute-done((f16[1,520,128]{2,1,0:T(8,128)(2,1)S(1)}, f16[1,520,128]{2,1,0:T(8,128)(2,1)S(1)}, u32[]{:S(2)}, u32[]{:S(2)}) %collective-permute-start.35) | collective-permute-done | bytes 133152 | tf_op jit(solution)/shard_map/ppermute | solution.py:249
  141.8 1.3 collective-permute-done.34
  143.1 0.6 collective-permute-done.33
  143.7 0.8 fusion.5
  (98 shorter events, 5.7 us)
Async XLA Ops:
  0.0 11.1 %copy-start.1 = (bf16[512,128]{1,0:T(8,128)(2,1)S(1)}, bf16[512,128]{1,0:T(8,128)(2,1)}, u32[]{:S(2)}) copy-start(bf16[512,128]{1,0:T(8,128)(2,1)} %param.4) | copy-start | bytes 393220
  0.0 12.6 %copy-start.2 = (s32[1,1,512]{2,1,0:T(1,128)S(1)}, s32[1,1,512]{2,1,0:T(1,128)}, u32[]{:S(2)}) copy-start(s32[1,1,512]{2,1,0:T(1,128)} %param.7) | copy-start | bytes 6148
  0.0 12.7 %copy-start = (s32[1,1,65]{2,1,0:T(1,128)S(1)}, s32[1,1,65]{2,1,0:T(1,128)}, u32[]{:S(2)}) copy-start(s32[1,1,65]{2,1,0:T(1,128)} %param.6) | copy-start | bytes 784
  0.0 7.7 %collective-permute-start.2 = (bf16[512,128]{1,0:T(8,128)(2,1)}, bf16[512,128]{1,0:T(8,128)(2,1)S(1)}, u32[]{:S(2)}, u32[]{:S(2)}) collective-permute-start(bf16[512,128]{1,0:T(8,128)(2,1)} %param.4), channel_id=1, source_target_pairs={{0,64},{16,80},{32,96},{48,112},{64,0},{80,16},{96,32},{112,48},{1... | collective-permute-start | bytes 393224 | tf_op jit(solution)/shard_map/ppermute | solution.py:240
  4.0 5.2 %collective-permute-start = (bf16[512,128]{1,0:T(8,128)(2,1)}, bf16[512,128]{1,0:T(8,128)(2,1)S(1)}, u32[]{:S(2)}, u32[]{:S(2)}) collective-permute-start(bf16[512,128]{1,0:T(8,128)(2,1)} %param.4), channel_id=1, source_target_pairs={{0,16},{16,32},{32,48},{48,0},{64,80},{80,96},{96,112},{112,64},{1... | collective-permute-start | bytes 393224 | tf_op jit(solution)/shard_map/ppermute | solution.py:240
  4.4 6.4 %collective-permute-start.1 = (bf16[512,128]{1,0:T(8,128)(2,1)}, bf16[512,128]{1,0:T(8,128)(2,1)S(1)}, u32[]{:S(2)}, u32[]{:S(2)}) collective-permute-start(bf16[512,128]{1,0:T(8,128)(2,1)} %param.4), channel_id=1, source_target_pairs={{0,48},{16,0},{32,16},{48,32},{64,112},{80,64},{96,80},{112,96},{1... | collective-permute-start | bytes 393224 | tf_op jit(solution)/shard_map/ppermute | solution.py:240
  10.9 8.0 %collective-permute-start.3 = (bf16[1024,128]{1,0:T(8,128)(2,1)S(1)}, bf16[1024,128]{1,0:T(8,128)(2,1)S(1)}, u32[]{:S(2)}, u32[]{:S(2)}) collective-permute-start(bf16[1024,128]{1,0:T(8,128)(2,1)S(1)} %get-tuple-element.33.after_ref), channel_id=1, source_target_pairs={{0,64},{16,80},{32,96},{48,112},{64,0},{80,16},{96,32},{112,48},{1... | collective-permute-start | bytes 786440 | tf_op jit(solution)/shard_map/ppermute | solution.py:240
  11.1 8.5 %collective-permute-start.4 = (bf16[1024,128]{1,0:T(8,128)(2,1)S(1)}, bf16[1024,128]{1,0:T(8,128)(2,1)S(1)}, u32[]{:S(2)}, u32[]{:S(2)}) collective-permute-start(bf16[1024,128]{1,0:T(8,128)(2,1)S(1)} %pad_maximum_fusion.3), channel_id=1, source_target_pairs={{0,32},{16,48},{32,0},{48,16},{64,96},{80,112},{96,64},{112,80},{1... | collective-permute-start | bytes 786440 | tf_op jit(solution)/shard_map/ppermute | solution.py:240
  23.0 2.7 %collective-permute-start.6 = (f32[16,128,128]{2,1,0:T(8,128)S(1)}, f32[16,128,128]{2,1,0:T(8,128)S(1)}, u32[]{:S(2)}, u32[]{:S(2)}) collective-permute-start(f32[16,128,128]{2,1,0:T(8,128)S(1)} %get-tuple-element.12), channel_id=1, source_target_pairs={{0,1},{1,0},{2,3},{3,2},{4,5},{5,4},{6,7},{7,6},{8,9},{9,8},{10,11... | collective-permute-start | bytes 3145736 | tf_op jit(solution)/shard_map/ppermute | solution.py:273
  26.2 10.0 %collective-permute-start.7 = (f16[2,520,128]{2,1,0:T(8,128)(2,1)S(1)}, f16[2,520,128]{2,1,0:T(8,128)(2,1)S(1)}, u32[]{:S(2)}, u32[]{:S(2)}) collective-permute-start(f16[2,520,128]{2,1,0:T(8,128)(2,1)S(1)} %get-tuple-element.30), channel_id=1, source_target_pairs={{0,4},{1,5},{2,6},{3,7},{4,0},{5,1},{6,2},{7,3},{8,12},{9,13},{10,... | collective-permute-start | bytes 798728 | tf_op jit(solution)/shard_map/ppermute | solution.py:249
  30.8 9.1 %collective-permute-start.5 = (f32[16,128,128]{2,1,0:T(8,128)S(1)}, f32[16,128,128]{2,1,0:T(8,128)S(1)}, u32[]{:S(2)}, u32[]{:S(2)}) collective-permute-start(f32[16,128,128]{2,1,0:T(8,128)S(1)} %some_terms.12), channel_id=1, source_target_pairs={{0,1},{1,0},{2,3},{3,2},{4,5},{5,4},{6,7},{7,6},{8,9},{9,8},{10,11... | collective-permute-start | bytes 3145736 | tf_op jit(solution)/shard_map/ppermute | solution.py:279
  30.9 8.8 %collective-permute-start.8 = (f16[2,520,128]{2,1,0:T(8,128)(2,1)S(1)}, f16[2,520,128]{2,1,0:T(8,128)(2,1)S(1)}, u32[]{:S(2)}, u32[]{:S(2)}) collective-permute-start(f16[2,520,128]{2,1,0:T(8,128)(2,1)S(1)} %get-tuple-element.31), channel_id=1, source_target_pairs={{0,8},{1,9},{2,10},{3,11},{4,12},{5,13},{6,14},{7,15},{8,0},{9,1},... | collective-permute-start | bytes 798728 | tf_op jit(solution)/shard_map/ppermute | solution.py:249
  40.4 5.2 %collective-permute-start.11 = (f16[1,520,128]{2,1,0:T(8,128)(2,1)S(1)}, f16[1,520,128]{2,1,0:T(8,128)(2,1)S(1)}, u32[]{:S(2)}, u32[]{:S(2)}) collective-permute-start(f16[1,520,128]{2,1,0:T(8,128)(2,1)S(1)} %get-tuple-element.28), channel_id=1, source_target_pairs={{0,6},{1,7},{2,0},{3,1},{4,2},{5,3},{6,4},{7,5},{8,14},{9,15},{10,... | collective-permute-start | bytes 399368 | tf_op jit(solution)/shard_map/ppermute | solution.py:249
  41.5 6.2 %collective-permute-start.10 = (f16[1,520,128]{2,1,0:T(8,128)(2,1)S(1)}, f16[1,520,128]{2,1,0:T(8,128)(2,1)S(1)}, u32[]{:S(2)}, u32[]{:S(2)}) collective-permute-start(f16[1,520,128]{2,1,0:T(8,128)(2,1)S(1)} %get-tuple-element.29), channel_id=1, source_target_pairs={{0,2},{1,3},{2,4},{3,5},{4,6},{5,7},{6,0},{7,1},{8,10},{9,11},{10,... | collective-permute-start | bytes 399368 | tf_op jit(solution)/shard_map/ppermute | solution.py:249
  42.5 5.2 %collective-permute-start.9 = (f16[1,520,128]{2,1,0:T(8,128)(2,1)S(1)}, f16[1,520,128]{2,1,0:T(8,128)(2,1)S(1)}, u32[]{:S(2)}, u32[]{:S(2)}) collective-permute-start(f16[1,520,128]{2,1,0:T(8,128)(2,1)S(1)} %get-tuple-element.27), channel_id=1, source_target_pairs={{0,8},{1,9},{2,10},{3,11},{4,12},{5,13},{6,14},{7,15},{8,0},{9,1},... | collective-permute-start | bytes 399368 | tf_op jit(solution)/shard_map/ppermute | solution.py:249
  47.9 9.4 %collective-permute-start.12 = (bf16[512,128]{1,0:T(8,128)(2,1)S(1)}, bf16[512,128]{1,0:T(8,128)(2,1)S(1)}, u32[]{:S(2)}, u32[]{:S(2)}) collective-permute-start(bf16[512,128]{1,0:T(8,128)(2,1)S(1)} %get-tuple-element.16), channel_id=1, source_target_pairs={{0,64},{16,80},{32,96},{48,112},{64,0},{80,16},{96,32},{112,48},{1... | collective-permute-start | bytes 393224 | tf_op jit(solution)/shard_map/ppermute | solution.py:240
  54.3 6.4 %collective-permute-start.13 = (bf16[512,128]{1,0:T(8,128)(2,1)S(1)}, bf16[512,128]{1,0:T(8,128)(2,1)S(1)}, u32[]{:S(2)}, u32[]{:S(2)}) collective-permute-start(bf16[512,128]{1,0:T(8,128)(2,1)S(1)} %get-tuple-element.16), channel_id=1, source_target_pairs={{0,16},{16,32},{32,48},{48,0},{64,80},{80,96},{96,112},{112,64},{1... | collective-permute-start | bytes 393224 | tf_op jit(solution)/shard_map/ppermute | solution.py:240
  54.3 11.7 %collective-permute-start.14 = (bf16[512,128]{1,0:T(8,128)(2,1)S(1)}, bf16[512,128]{1,0:T(8,128)(2,1)S(1)}, u32[]{:S(2)}, u32[]{:S(2)}) collective-permute-start(bf16[512,128]{1,0:T(8,128)(2,1)S(1)} %get-tuple-element.16), channel_id=1, source_target_pairs={{0,48},{16,0},{32,16},{48,32},{64,112},{80,64},{96,80},{112,96},{1... | collective-permute-start | bytes 393224 | tf_op jit(solution)/shard_map/ppermute | solution.py:240
  57.3 16.7 %collective-permute-start.16 = (bf16[1024,128]{1,0:T(8,128)(2,1)S(1)}, bf16[1024,128]{1,0:T(8,128)(2,1)S(1)}, u32[]{:S(2)}, u32[]{:S(2)}) collective-permute-start(bf16[1024,128]{1,0:T(8,128)(2,1)S(1)} %pad_maximum_fusion.5), channel_id=1, source_target_pairs={{0,32},{16,48},{32,0},{48,16},{64,96},{80,112},{96,64},{112,80},{1... | collective-permute-start | bytes 786440 | tf_op jit(solution)/shard_map/ppermute | solution.py:240
  66.0 8.0 %collective-permute-start.15 = (bf16[1024,128]{1,0:T(8,128)(2,1)S(1)}, bf16[1024,128]{1,0:T(8,128)(2,1)S(1)}, u32[]{:S(2)}, u32[]{:S(2)}) collective-permute-start(bf16[1024,128]{1,0:T(8,128)(2,1)S(1)} %pad_maximum_fusion.4), channel_id=1, source_target_pairs={{0,64},{16,80},{32,96},{48,112},{64,0},{80,16},{96,32},{112,48},{1... | collective-permute-start | bytes 786440 | tf_op jit(solution)/shard_map/ppermute | solution.py:240
  75.3 2.7 %collective-permute-start.18 = (f32[16,128,128]{2,1,0:T(8,128)S(1)}, f32[16,128,128]{2,1,0:T(8,128)S(1)}, u32[]{:S(2)}, u32[]{:S(2)}) collective-permute-start(f32[16,128,128]{2,1,0:T(8,128)S(1)} %some_terms.17), channel_id=1, source_target_pairs={{0,1},{1,0},{2,3},{3,2},{4,5},{5,4},{6,7},{7,6},{8,9},{9,8},{10,11... | collective-permute-start | bytes 3145736 | tf_op jit(solution)/shard_map/ppermute | solution.py:273
  78.6 10.0 %collective-permute-start.19 = (f16[2,520,128]{2,1,0:T(8,128)(2,1)S(1)}, f16[2,520,128]{2,1,0:T(8,128)(2,1)S(1)}, u32[]{:S(2)}, u32[]{:S(2)}) collective-permute-start(f16[2,520,128]{2,1,0:T(8,128)(2,1)S(1)} %get-tuple-element.25), channel_id=1, source_target_pairs={{0,4},{1,5},{2,6},{3,7},{4,0},{5,1},{6,2},{7,3},{8,12},{9,13},{10,... | collective-permute-start | bytes 798728 | tf_op jit(solution)/shard_map/ppermute | solution.py:249
  80.5 9.1 %collective-permute-start.17 = (f32[16,128,128]{2,1,0:T(8,128)S(1)}, f32[16,128,128]{2,1,0:T(8,128)S(1)}, u32[]{:S(2)}, u32[]{:S(2)}) collective-permute-start(f32[16,128,128]{2,1,0:T(8,128)S(1)} %some_terms.15), channel_id=1, source_target_pairs={{0,1},{1,0},{2,3},{3,2},{4,5},{5,4},{6,7},{7,6},{8,9},{9,8},{10,11... | collective-permute-start | bytes 3145736 | tf_op jit(solution)/shard_map/ppermute | solution.py:279
  80.6 8.8 %collective-permute-start.20 = (f16[2,520,128]{2,1,0:T(8,128)(2,1)S(1)}, f16[2,520,128]{2,1,0:T(8,128)(2,1)S(1)}, u32[]{:S(2)}, u32[]{:S(2)}) collective-permute-start(f16[2,520,128]{2,1,0:T(8,128)(2,1)S(1)} %get-tuple-element.26), channel_id=1, source_target_pairs={{0,8},{1,9},{2,10},{3,11},{4,12},{5,13},{6,14},{7,15},{8,0},{9,1},... | collective-permute-start | bytes 798728 | tf_op jit(solution)/shard_map/ppermute | solution.py:249
  90.1 5.8 %collective-permute-start.23 = (f16[1,520,128]{2,1,0:T(8,128)(2,1)S(1)}, f16[1,520,128]{2,1,0:T(8,128)(2,1)S(1)}, u32[]{:S(2)}, u32[]{:S(2)}) collective-permute-start(f16[1,520,128]{2,1,0:T(8,128)(2,1)S(1)} %get-tuple-element.23), channel_id=1, source_target_pairs={{0,6},{1,7},{2,0},{3,1},{4,2},{5,3},{6,4},{7,5},{8,14},{9,15},{10,... | collective-permute-start | bytes 399368 | tf_op jit(solution)/shard_map/ppermute | solution.py:249
  92.8 6.2 %collective-permute-start.22 = (f16[1,520,128]{2,1,0:T(8,128)(2,1)S(1)}, f16[1,520,128]{2,1,0:T(8,128)(2,1)S(1)}, u32[]{:S(2)}, u32[]{:S(2)}) collective-permute-start(f16[1,520,128]{2,1,0:T(8,128)(2,1)S(1)} %get-tuple-element.24), channel_id=1, source_target_pairs={{0,2},{1,3},{2,4},{3,5},{4,6},{5,7},{6,0},{7,1},{8,10},{9,11},{10,... | collective-permute-start | bytes 399368 | tf_op jit(solution)/shard_map/ppermute | solution.py:249
  92.8 6.2 %collective-permute-start.21 = (f16[1,520,128]{2,1,0:T(8,128)(2,1)S(1)}, f16[1,520,128]{2,1,0:T(8,128)(2,1)S(1)}, u32[]{:S(2)}, u32[]{:S(2)}) collective-permute-start(f16[1,520,128]{2,1,0:T(8,128)(2,1)S(1)} %get-tuple-element.22), channel_id=1, source_target_pairs={{0,8},{1,9},{2,10},{3,11},{4,12},{5,13},{6,14},{7,15},{8,0},{9,1},... | collective-permute-start | bytes 399368 | tf_op jit(solution)/shard_map/ppermute | solution.py:249
  99.1 6.6 %collective-permute-start.24 = (bf16[512,128]{1,0:T(8,128)(2,1)S(1)}, bf16[512,128]{1,0:T(8,128)(2,1)S(1)}, u32[]{:S(2)}, u32[]{:S(2)}) collective-permute-start(bf16[512,128]{1,0:T(8,128)(2,1)S(1)} %get-tuple-element.14), channel_id=1, source_target_pairs={{0,64},{16,80},{32,96},{48,112},{64,0},{80,16},{96,32},{112,48},{1... | collective-permute-start | bytes 393224 | tf_op jit(solution)/shard_map/ppermute | solution.py:240
  100.5 6.3 %collective-permute-start.25 = (bf16[512,128]{1,0:T(8,128)(2,1)S(1)}, bf16[512,128]{1,0:T(8,128)(2,1)S(1)}, u32[]{:S(2)}, u32[]{:S(2)}) collective-permute-start(bf16[512,128]{1,0:T(8,128)(2,1)S(1)} %get-tuple-element.14), channel_id=1, source_target_pairs={{0,16},{16,32},{32,48},{48,0},{64,80},{80,96},{96,112},{112,64},{1... | collective-permute-start | bytes 393224 | tf_op jit(solution)/shard_map/ppermute | solution.py:240
  100.5 6.3 %collective-permute-start.26 = (bf16[512,128]{1,0:T(8,128)(2,1)S(1)}, bf16[512,128]{1,0:T(8,128)(2,1)S(1)}, u32[]{:S(2)}, u32[]{:S(2)}) collective-permute-start(bf16[512,128]{1,0:T(8,128)(2,1)S(1)} %get-tuple-element.14), channel_id=1, source_target_pairs={{0,48},{16,0},{32,16},{48,32},{64,112},{80,64},{96,80},{112,96},{1... | collective-permute-start | bytes 393224 | tf_op jit(solution)/shard_map/ppermute | solution.py:240
  105.7 10.5 %collective-permute-start.28 = (bf16[1024,128]{1,0:T(8,128)(2,1)S(1)}, bf16[1024,128]{1,0:T(8,128)(2,1)S(1)}, u32[]{:S(2)}, u32[]{:S(2)}) collective-permute-start(bf16[1024,128]{1,0:T(8,128)(2,1)S(1)} %pad_maximum_fusion.7), channel_id=1, source_target_pairs={{0,32},{16,48},{32,0},{48,16},{64,96},{80,112},{96,64},{112,80},{1... | collective-permute-start | bytes 786440 | tf_op jit(solution)/shard_map/ppermute | solution.py:240
  106.9 9.3 %collective-permute-start.27 = (bf16[1024,128]{1,0:T(8,128)(2,1)S(1)}, bf16[1024,128]{1,0:T(8,128)(2,1)S(1)}, u32[]{:S(2)}, u32[]{:S(2)}) collective-permute-start(bf16[1024,128]{1,0:T(8,128)(2,1)S(1)} %pad_maximum_fusion.6), channel_id=1, source_target_pairs={{0,64},{16,80},{32,96},{48,112},{64,0},{80,16},{96,32},{112,48},{1... | collective-permute-start | bytes 786440 | tf_op jit(solution)/shard_map/ppermute | solution.py:240
  117.6 2.7 %collective-permute-start.30 = (f32[16,128,128]{2,1,0:T(8,128)S(1)}, f32[16,128,128]{2,1,0:T(8,128)S(1)}, u32[]{:S(2)}, u32[]{:S(2)}) collective-permute-start(f32[16,128,128]{2,1,0:T(8,128)S(1)} %some_terms.21), channel_id=1, source_target_pairs={{0,1},{1,0},{2,3},{3,2},{4,5},{5,4},{6,7},{7,6},{8,9},{9,8},{10,11... | collective-permute-start | bytes 3145736 | tf_op jit(solution)/shard_map/ppermute | solution.py:273
  120.8 11.7 %collective-permute-start.31 = (f16[2,520,128]{2,1,0:T(8,128)(2,1)S(1)}, f16[2,520,128]{2,1,0:T(8,128)(2,1)S(1)}, u32[]{:S(2)}, u32[]{:S(2)}) collective-permute-start(f16[2,520,128]{2,1,0:T(8,128)(2,1)S(1)} %get-tuple-element.20), channel_id=1, source_target_pairs={{0,4},{1,5},{2,6},{3,7},{4,0},{5,1},{6,2},{7,3},{8,12},{9,13},{10,... | collective-permute-start | bytes 798728 | tf_op jit(solution)/shard_map/ppermute | solution.py:249
  127.0 9.1 %collective-permute-start.29 = (f32[16,128,128]{2,1,0:T(8,128)S(1)}, f32[16,128,128]{2,1,0:T(8,128)S(1)}, u32[]{:S(2)}, u32[]{:S(2)}) collective-permute-start(f32[16,128,128]{2,1,0:T(8,128)S(1)} %some_terms.19), channel_id=1, source_target_pairs={{0,1},{1,0},{2,3},{3,2},{4,5},{5,4},{6,7},{7,6},{8,9},{9,8},{10,11... | collective-permute-start | bytes 3145736 | tf_op jit(solution)/shard_map/ppermute | solution.py:279
  127.1 8.8 %collective-permute-start.32 = (f16[2,520,128]{2,1,0:T(8,128)(2,1)S(1)}, f16[2,520,128]{2,1,0:T(8,128)(2,1)S(1)}, u32[]{:S(2)}, u32[]{:S(2)}) collective-permute-start(f16[2,520,128]{2,1,0:T(8,128)(2,1)S(1)} %get-tuple-element.21), channel_id=1, source_target_pairs={{0,8},{1,9},{2,10},{3,11},{4,12},{5,13},{6,14},{7,15},{8,0},{9,1},... | collective-permute-start | bytes 798728 | tf_op jit(solution)/shard_map/ppermute | solution.py:249
  136.6 5.2 %collective-permute-start.35 = (f16[1,520,128]{2,1,0:T(8,128)(2,1)S(1)}, f16[1,520,128]{2,1,0:T(8,128)(2,1)S(1)}, u32[]{:S(2)}, u32[]{:S(2)}) collective-permute-start(f16[1,520,128]{2,1,0:T(8,128)(2,1)S(1)} %get-tuple-element.18), channel_id=1, source_target_pairs={{0,6},{1,7},{2,0},{3,1},{4,2},{5,3},{6,4},{7,5},{8,14},{9,15},{10,... | collective-permute-start | bytes 399368 | tf_op jit(solution)/shard_map/ppermute | solution.py:249
  136.7 6.4 %collective-permute-start.34 = (f16[1,520,128]{2,1,0:T(8,128)(2,1)S(1)}, f16[1,520,128]{2,1,0:T(8,128)(2,1)S(1)}, u32[]{:S(2)}, u32[]{:S(2)}) collective-permute-start(f16[1,520,128]{2,1,0:T(8,128)(2,1)S(1)} %get-tuple-element.19), channel_id=1, source_target_pairs={{0,2},{1,3},{2,4},{3,5},{4,6},{5,7},{6,0},{7,1},{8,10},{9,11},{10,... | collective-permute-start | bytes 399368 | tf_op jit(solution)/shard_map/ppermute | solution.py:249
  138.7 5.0 %collective-permute-start.33 = (f16[1,520,128]{2,1,0:T(8,128)(2,1)S(1)}, f16[1,520,128]{2,1,0:T(8,128)(2,1)S(1)}, u32[]{:S(2)}, u32[]{:S(2)}) collective-permute-start(f16[1,520,128]{2,1,0:T(8,128)(2,1)S(1)} %get-tuple-element.17), channel_id=1, source_target_pairs={{0,8},{1,9},{2,10},{3,11},{4,12},{5,13},{6,14},{7,15},{8,0},{9,1},... | collective-permute-start | bytes 399368 | tf_op jit(solution)/shard_map/ppermute | solution.py:249

commit v2 on v1

--- a/solution.py
+++ b/solution.py
@@ -160,7 +160,7 @@
         out_shape=jax.ShapeDtypeStruct((rows, size, vector.shape[2]), jnp.float32),
         compiler_params=pltpu.CompilerParams(vmem_limit_bytes=24 * MIB),
         cost_estimate=pl.CostEstimate(
-            flops=2 * rows * 8 * size**3, bytes_accessed=rows * 8 * size * size, transcendentals=0
+            flops=2 * rows * 64 * size**3, bytes_accessed=rows * 8 * size * size, transcendentals=0
         ),
         name="some_terms",
     )(words, counts, vector, pltpu.with_memory_space_constraint(held, pltpu.VMEM))

time: 146 us -> 144 us (0.986); the launches traced: 145 us -> 141 us
  waiting for transfers between devices: 70.4 us -> 61.4 us
  starting transfers between devices: 45.7 us -> 51.1 us
    ppermute x15, waiting for transfers between devices: 32.2 us -> 27.2 us  [shift(): return lax.ppermute(x, 'row', pairs)]
    ppermute x15, starting transfers between devices: 20.4 us -> 24.4 us  [pass_on(): return lax.ppermute(x, 'col', pairs)]
    ppermute x6, waiting for transfers between devices: 3.93 us -> 0.18 us  [multiply(): taken = lax.ppermute(given, 'col', swap)]
  transfers between devices with their start and end apart: 36 -> 36, of which waited for: 28 -> 25; matrix products, arithmetic and copies ran while one was open for 1% -> 1% of each run, Pallas kernels for 11% -> 11%
where the time goes in v2:
time: 144 us; the launch traced here: 141 us
  waiting for transfers between devices  61.4 us (43%)
  starting transfers between devices  51.1 us (35%)
  Pallas kernels  23.6 us (16%)
  other arithmetic  2.18 us (2%)
  local copies, waits for them, and re-layouts  1.94 us (1%)
    ppermute x15, waiting for transfers between devices, pass_on(): return lax.ppermute(x, 'col', pairs)  34.1 us
    ppermute x15, waiting for transfers between devices, shift(): return lax.ppermute(x, 'row', pairs)  27.2 us
    ppermute x15, starting transfers between devices, shift(): return lax.ppermute(x, 'row', pairs)  26.1 us
    ppermute x15, starting transfers between devices, pass_on(): return lax.ppermute(x, 'col', pairs)  24.4 us
    pallas_call x11, Pallas kernels, some_terms(): pl.pallas_call(functools.partial(some_kernel, index=index, height=height)...  14.2 us
    pallas_call x1, Pallas kernels, make_lists(): pl.pallas_call(functools.partial(pair_list, height=height), in_specs=[sme...  4.19 us
    pallas_call x1, Pallas kernels, first_terms(): pl.pallas_call(functools.partial(first_kernel, height=height), in_specs=[...  3.3 us
  transfers between devices with their start and end apart: 36, of which 25 were waited for; matrix products, arithmetic and copies ran while one was open for 1% of the time, Pallas kernels for 11%

profile of v2, /device:TPU:6, one launch (start us, length us, event | category | flops | bytes accessed | tf_op | source)
XLA Modules:
  0.0 141.0 jit_solution(6706760108202621386)
XLA Ops:
  0.0 4.0 %collective-permute-start.2 = (bf16[512,128]{1,0:T(8,128)(2,1)}, bf16[512,128]{1,0:T(8,128)(2,1)S(1)}, u32[]{:S(2)}, u32[]{:S(2)}) collective-permute-start(bf16[512,128]{1,0:T(8,128)(2,1)} %param.4), channel_id=1, source_target_pairs={{0,64},{16,80},{32,96},{48,112},{64,0},{80,16},{96,32},{112,48},{1... | collective-permute-start | bytes 393224 | tf_op jit(solution)/shard_map/ppermute | solution.py:240
  4.0 0.5 collective-permute-start
  4.4 1.5 %collective-permute-start.1 = (bf16[512,128]{1,0:T(8,128)(2,1)}, bf16[512,128]{1,0:T(8,128)(2,1)S(1)}, u32[]{:S(2)}, u32[]{:S(2)}) collective-permute-start(bf16[512,128]{1,0:T(8,128)(2,1)} %param.4), channel_id=1, source_target_pairs={{0,48},{16,0},{32,16},{48,32},{64,112},{80,64},{96,80},{112,96},{1... | collective-permute-start | bytes 393224 | tf_op jit(solution)/shard_map/ppermute | solution.py:240
  6.0 0.9 constant_dynamic-update-slice_fusion.7
  7.0 0.7 collective-permute-done.2
  7.7 1.4 %collective-permute-done = bf16[512,128]{1,0:T(8,128)(2,1)S(1)} collective-permute-done((bf16[512,128]{1,0:T(8,128)(2,1)}, bf16[512,128]{1,0:T(8,128)(2,1)S(1)}, u32[]{:S(2)}, u32[]{:S(2)}) %collective-permute-start) | collective-permute-done | bytes 131104 | tf_op jit(solution)/shard_map/ppermute | solution.py:240
  9.2 1.7 %collective-permute-done.1 = bf16[512,128]{1,0:T(8,128)(2,1)S(1)} collective-permute-done((bf16[512,128]{1,0:T(8,128)(2,1)}, bf16[512,128]{1,0:T(8,128)(2,1)S(1)}, u32[]{:S(2)}, u32[]{:S(2)}) %collective-permute-start.1) | collective-permute-done | bytes 131104 | tf_op jit(solution)/shard_map/ppermute | solution.py:240
  11.1 1.5 %collective-permute-start.4 = (bf16[1024,128]{1,0:T(8,128)(2,1)S(1)}, bf16[1024,128]{1,0:T(8,128)(2,1)S(1)}, u32[]{:S(2)}, u32[]{:S(2)}) collective-permute-start(bf16[1024,128]{1,0:T(8,128)(2,1)S(1)} %pad_maximum_fusion.3), channel_id=1, source_target_pairs={{0,32},{16,48},{32,0},{48,16},{64,96},{80,112},{96,64},{112,80},{1... | collective-permute-start | bytes 786440 | tf_op jit(solution)/shard_map/ppermute | solution.py:240
  12.7 4.2 %pair_list.1 = (s32[4,120]{1,0:T(4,128)S(1)}, s32[4]{0:T(128)S(1)}) custom-call(s32[1]{0:T(128)} %bitcast.core_ref, s32[8]{0:T(128)S(1)} %fusion.38.order_ref, s32[65]{0:T(128)S(1)} %bitcast.69, s32[512]{0:T(512)S(1)} %fusion.21.column_ref, bf16[1024,128]{1,0:T(8,128)(2,1)S(1)} %get-tuple-element.33.after_ref), custom_call_target="tpu_custom_call" | custom-call | tf_op jit(solution)/shard_map/pair_list/pallas_call | solution.py:55
  16.9 1.9 %collective-permute-done.3 = bf16[1024,128]{1,0:T(8,128)(2,1)S(1)} collective-permute-done((bf16[1024,128]{1,0:T(8,128)(2,1)S(1)}, bf16[1024,128]{1,0:T(8,128)(2,1)S(1)}, u32[]{:S(2)}, u32[]{:S(2)}) %collective-permute-start.3) | collective-permute-done | bytes 262176 | tf_op jit(solution)/shard_map/ppermute | solution.py:240
  18.9 0.8 collective-permute-done.4
  19.7 3.3 %first_terms.1 = (f32[16,128,128]{2,1,0:T(8,128)S(1)}, bf16[512,128,128]{2,1,0:T(8,128)(2,1)S(1)}) custom-call(s32[8]{0:T(128)S(1)} %fusion.38.order_ref, s32[65]{0:T(128)S(1)} %bitcast.70, s32[4,120]{1,0:T(4,128)S(1)} %get-tuple-element.9.word_ref, s32[4]{0:T(128)S(1)} %get-tuple-element.10.count_ref, bf16[32,128,128]{2,1,0:T(8,128)(2,1)S(1)} %bitcast.62, ...), custom_call_target="tpu_custom_call" | custom-call | tf_op jit(solution)/shard_map/first_terms/pallas_call | solution.py:138
  23.1 1.3 some_terms.13.refs_0_
  24.3 1.3 some_terms.12
  25.7 0.3 combine.6
  26.2 9.3 %collective-permute-start.7 = (f16[2,520,128]{2,1,0:T(8,128)(2,1)S(1)}, f16[2,520,128]{2,1,0:T(8,128)(2,1)S(1)}, u32[]{:S(2)}, u32[]{:S(2)}) collective-permute-start(f16[2,520,128]{2,1,0:T(8,128)(2,1)S(1)} %get-tuple-element.30), channel_id=1, source_target_pairs={{0,4},{1,5},{2,6},{3,7},{4,0},{5,1},{6,2},{7,3},{8,12},{9,13},{10,... | collective-permute-start | bytes 798728 | tf_op jit(solution)/shard_map/ppermute | solution.py:249
  35.6 1.3 some_terms.11.refs_0_
  36.9 3.1 %collective-permute-done.7 = f16[2,520,128]{2,1,0:T(8,128)(2,1)S(1)} collective-permute-done((f16[2,520,128]{2,1,0:T(8,128)(2,1)S(1)}, f16[2,520,128]{2,1,0:T(8,128)(2,1)S(1)}, u32[]{:S(2)}, u32[]{:S(2)}) %collective-permute-start.7) | collective-permute-done | bytes 266272 | tf_op jit(solution)/shard_map/ppermute | solution.py:249
  40.1 1.9 %collective-permute-done.8 = f16[2,520,128]{2,1,0:T(8,128)(2,1)S(1)} collective-permute-done((f16[2,520,128]{2,1,0:T(8,128)(2,1)S(1)}, f16[2,520,128]{2,1,0:T(8,128)(2,1)S(1)}, u32[]{:S(2)}, u32[]{:S(2)}) %collective-permute-start.8) | collective-permute-done | bytes 266272 | tf_op jit(solution)/shard_map/ppermute | solution.py:249
  42.2 0.3 combine.7
  42.8 2.0 %collective-permute-start.10 = (f16[1,520,128]{2,1,0:T(8,128)(2,1)S(1)}, f16[1,520,128]{2,1,0:T(8,128)(2,1)S(1)}, u32[]{:S(2)}, u32[]{:S(2)}) collective-permute-start(f16[1,520,128]{2,1,0:T(8,128)(2,1)S(1)} %get-tuple-element.29), channel_id=1, source_target_pairs={{0,2},{1,3},{2,4},{3,5},{4,6},{5,7},{6,0},{7,1},{8,10},{9,11},{10,... | collective-permute-start | bytes 399368 | tf_op jit(solution)/shard_map/ppermute | solution.py:249
  44.8 3.0 %collective-permute-done.11 = f16[1,520,128]{2,1,0:T(8,128)(2,1)S(1)} collective-permute-done((f16[1,520,128]{2,1,0:T(8,128)(2,1)S(1)}, f16[1,520,128]{2,1,0:T(8,128)(2,1)S(1)}, u32[]{:S(2)}, u32[]{:S(2)}) %collective-permute-start.11) | collective-permute-done | bytes 133152 | tf_op jit(solution)/shard_map/ppermute | solution.py:249
  47.7 1.3 collective-permute-done.10
  49.0 0.7 collective-permute-done.9
  49.9 3.5 %collective-permute-start.12 = (bf16[512,128]{1,0:T(8,128)(2,1)S(1)}, bf16[512,128]{1,0:T(8,128)(2,1)S(1)}, u32[]{:S(2)}, u32[]{:S(2)}) collective-permute-start(bf16[512,128]{1,0:T(8,128)(2,1)S(1)} %get-tuple-element.16), channel_id=1, source_target_pairs={{0,64},{16,80},{32,96},{48,112},{64,0},{80,16},{96,32},{112,48},{1... | collective-permute-start | bytes 393224 | tf_op jit(solution)/shard_map/ppermute | solution.py:240
  53.3 2.0 %collective-permute-start.14 = (bf16[512,128]{1,0:T(8,128)(2,1)S(1)}, bf16[512,128]{1,0:T(8,128)(2,1)S(1)}, u32[]{:S(2)}, u32[]{:S(2)}) collective-permute-start(bf16[512,128]{1,0:T(8,128)(2,1)S(1)} %get-tuple-element.16), channel_id=1, source_target_pairs={{0,48},{16,0},{32,16},{48,32},{64,112},{80,64},{96,80},{112,96},{1... | collective-permute-start | bytes 393224 | tf_op jit(solution)/shard_map/ppermute | solution.py:240
  55.4 1.1 collective-permute-done.12
  56.4 1.6 %collective-permute-start.16 = (bf16[1024,128]{1,0:T(8,128)(2,1)S(1)}, bf16[1024,128]{1,0:T(8,128)(2,1)S(1)}, u32[]{:S(2)}, u32[]{:S(2)}) collective-permute-start(bf16[1024,128]{1,0:T(8,128)(2,1)S(1)} %pad_maximum_fusion.5), channel_id=1, source_target_pairs={{0,32},{16,48},{32,0},{48,16},{64,96},{80,112},{96,64},{112,80},{1... | collective-permute-start | bytes 786440 | tf_op jit(solution)/shard_map/ppermute | solution.py:240
  58.0 0.7 collective-permute-done.13
  58.7 2.7 %collective-permute-done.14 = bf16[512,128]{1,0:T(8,128)(2,1)S(1)} collective-permute-done((bf16[512,128]{1,0:T(8,128)(2,1)S(1)}, bf16[512,128]{1,0:T(8,128)(2,1)S(1)}, u32[]{:S(2)}, u32[]{:S(2)}) %collective-permute-start.14) | collective-permute-done | bytes 131104 | tf_op jit(solution)/shard_map/ppermute | solution.py:240
  61.7 7.6 %collective-permute-done.15 = bf16[1024,128]{1,0:T(8,128)(2,1)S(1)} collective-permute-done((bf16[1024,128]{1,0:T(8,128)(2,1)S(1)}, bf16[1024,128]{1,0:T(8,128)(2,1)S(1)}, u32[]{:S(2)}, u32[]{:S(2)}) %collective-permute-start.15) | collective-permute-done | bytes 262176 | tf_op jit(solution)/shard_map/ppermute | solution.py:240
  69.4 1.3 some_terms.17
  70.8 1.5 %some_terms.16.refs_0_ = f32[16,128,128]{2,1,0:T(8,128)S(1)} custom-call(s32[4,120]{1,0:T(4,128)S(1)} %get-tuple-element.9.word_ref, s32[4]{0:T(128)S(1)} %get-tuple-element.10.count_ref, bf16[32,128,128]{2,1,0:T(8,128)(2,1)S(1)} %bitcast.55, bf16[512,128,128]{2,1,0:T(8,128)(2,1)S(1)} %get-tuple-element.11.block_ref), custom_call_target="tpu_custom_call" | custom-call | flops 4294967296 | bytes 2097152 | tf_op jit(solution)/shard_map/some_terms/pallas_call | solution.py:156
  72.3 1.3 some_terms.15
  73.6 0.3 combine.8
  74.1 4.1 %collective-permute-start.19 = (f16[2,520,128]{2,1,0:T(8,128)(2,1)S(1)}, f16[2,520,128]{2,1,0:T(8,128)(2,1)S(1)}, u32[]{:S(2)}, u32[]{:S(2)}) collective-permute-start(f16[2,520,128]{2,1,0:T(8,128)(2,1)S(1)} %get-tuple-element.25), channel_id=1, source_target_pairs={{0,4},{1,5},{2,6},{3,7},{4,0},{5,1},{6,2},{7,3},{8,12},{9,13},{10,... | collective-permute-start | bytes 798728 | tf_op jit(solution)/shard_map/ppermute | solution.py:249
  78.1 1.0 collective-permute-start.20
  79.2 1.3 some_terms.14.refs_0_
  80.5 3.9 %collective-permute-done.19 = f16[2,520,128]{2,1,0:T(8,128)(2,1)S(1)} collective-permute-done((f16[2,520,128]{2,1,0:T(8,128)(2,1)S(1)}, f16[2,520,128]{2,1,0:T(8,128)(2,1)S(1)}, u32[]{:S(2)}, u32[]{:S(2)}) %collective-permute-start.19) | collective-permute-done | bytes 266272 | tf_op jit(solution)/shard_map/ppermute | solution.py:249
  84.4 1.5 %collective-permute-done.20 = f16[2,520,128]{2,1,0:T(8,128)(2,1)S(1)} collective-permute-done((f16[2,520,128]{2,1,0:T(8,128)(2,1)S(1)}, f16[2,520,128]{2,1,0:T(8,128)(2,1)S(1)}, u32[]{:S(2)}, u32[]{:S(2)}) %collective-permute-start.20) | collective-permute-done | bytes 266272 | tf_op jit(solution)/shard_map/ppermute | solution.py:249
  86.1 0.3 combine.9
  86.6 3.6 %collective-permute-start.23 = (f16[1,520,128]{2,1,0:T(8,128)(2,1)S(1)}, f16[1,520,128]{2,1,0:T(8,128)(2,1)S(1)}, u32[]{:S(2)}, u32[]{:S(2)}) collective-permute-start(f16[1,520,128]{2,1,0:T(8,128)(2,1)S(1)} %get-tuple-element.23), channel_id=1, source_target_pairs={{0,6},{1,7},{2,0},{3,1},{4,2},{5,3},{6,4},{7,5},{8,14},{9,15},{10,... | collective-permute-start | bytes 399368 | tf_op jit(solution)/shard_map/ppermute | solution.py:249
  90.3 0.3 collective-permute-start.21
  90.6 2.3 %collective-permute-done.23 = f16[1,520,128]{2,1,0:T(8,128)(2,1)S(1)} collective-permute-done((f16[1,520,128]{2,1,0:T(8,128)(2,1)S(1)}, f16[1,520,128]{2,1,0:T(8,128)(2,1)S(1)}, u32[]{:S(2)}, u32[]{:S(2)}) %collective-permute-start.23) | collective-permute-done | bytes 133152 | tf_op jit(solution)/shard_map/ppermute | solution.py:249
  92.8 3.6 %collective-permute-done.22 = f16[1,520,128]{2,1,0:T(8,128)(2,1)S(1)} collective-permute-done((f16[1,520,128]{2,1,0:T(8,128)(2,1)S(1)}, f16[1,520,128]{2,1,0:T(8,128)(2,1)S(1)}, u32[]{:S(2)}, u32[]{:S(2)}) %collective-permute-start.22) | collective-permute-done | bytes 133152 | tf_op jit(solution)/shard_map/ppermute | solution.py:249
  96.8 2.0 %collective-permute-start.26 = (bf16[512,128]{1,0:T(8,128)(2,1)S(1)}, bf16[512,128]{1,0:T(8,128)(2,1)S(1)}, u32[]{:S(2)}, u32[]{:S(2)}) collective-permute-start(bf16[512,128]{1,0:T(8,128)(2,1)S(1)} %get-tuple-element.14), channel_id=1, source_target_pairs={{0,48},{16,0},{32,16},{48,32},{64,112},{80,64},{96,80},{112,96},{1... | collective-permute-start | bytes 393224 | tf_op jit(solution)/shard_map/ppermute | solution.py:240
  98.8 4.4 %collective-permute-done.24 = bf16[512,128]{1,0:T(8,128)(2,1)S(1)} collective-permute-done((bf16[512,128]{1,0:T(8,128)(2,1)S(1)}, bf16[512,128]{1,0:T(8,128)(2,1)S(1)}, u32[]{:S(2)}, u32[]{:S(2)}) %collective-permute-start.24) | collective-permute-done | bytes 131104 | tf_op jit(solution)/shard_map/ppermute | solution.py:240
  103.3 8.8 %collective-permute-start.27 = (bf16[1024,128]{1,0:T(8,128)(2,1)S(1)}, bf16[1024,128]{1,0:T(8,128)(2,1)S(1)}, u32[]{:S(2)}, u32[]{:S(2)}) collective-permute-start(bf16[1024,128]{1,0:T(8,128)(2,1)S(1)} %pad_maximum_fusion.6), channel_id=1, source_target_pairs={{0,64},{16,80},{32,96},{48,112},{64,0},{80,16},{96,32},{112,48},{1... | collective-permute-start | bytes 786440 | tf_op jit(solution)/shard_map/ppermute | solution.py:240
  112.2 4.3 %collective-permute-done.27 = bf16[1024,128]{1,0:T(8,128)(2,1)S(1)} collective-permute-done((bf16[1024,128]{1,0:T(8,128)(2,1)S(1)}, bf16[1024,128]{1,0:T(8,128)(2,1)S(1)}, u32[]{:S(2)}, u32[]{:S(2)}) %collective-permute-start.27) | collective-permute-done | bytes 262176 | tf_op jit(solution)/shard_map/ppermute | solution.py:240
  116.6 1.3 some_terms.21
  118.0 1.3 some_terms.20.refs_0_
  119.2 1.3 some_terms.19
  120.6 0.3 combine.10
  121.1 0.3 collective-permute-start.31
  121.4 0.7 collective-permute-start.32
  122.1 1.3 some_terms.18.refs_0_
  123.7 7.8 %collective-permute-done.31 = f16[2,520,128]{2,1,0:T(8,128)(2,1)S(1)} collective-permute-done((f16[2,520,128]{2,1,0:T(8,128)(2,1)S(1)}, f16[2,520,128]{2,1,0:T(8,128)(2,1)S(1)}, u32[]{:S(2)}, u32[]{:S(2)}) %collective-permute-start.31) | collective-permute-done | bytes 266272 | tf_op jit(solution)/shard_map/ppermute | solution.py:249
  131.6 0.3 combine.11
  132.1 1.8 %collective-permute-start.35 = (f16[1,520,128]{2,1,0:T(8,128)(2,1)S(1)}, f16[1,520,128]{2,1,0:T(8,128)(2,1)S(1)}, u32[]{:S(2)}, u32[]{:S(2)}) collective-permute-start(f16[1,520,128]{2,1,0:T(8,128)(2,1)S(1)} %get-tuple-element.18), channel_id=1, source_target_pairs={{0,6},{1,7},{2,0},{3,1},{4,2},{5,3},{6,4},{7,5},{8,14},{9,15},{10,... | collective-permute-start | bytes 399368 | tf_op jit(solution)/shard_map/ppermute | solution.py:249
  133.9 0.3 collective-permute-start.34
  134.2 0.9 collective-permute-start.33
  135.1 2.2 %collective-permute-done.35 = f16[1,520,128]{2,1,0:T(8,128)(2,1)S(1)} collective-permute-done((f16[1,520,128]{2,1,0:T(8,128)(2,1)S(1)}, f16[1,520,128]{2,1,0:T(8,128)(2,1)S(1)}, u32[]{:S(2)}, u32[]{:S(2)}) %collective-permute-start.35) | collective-permute-done | bytes 133152 | tf_op jit(solution)/shard_map/ppermute | solution.py:249
  137.3 2.8 %collective-permute-done.34 = f16[1,520,128]{2,1,0:T(8,128)(2,1)S(1)} collective-permute-done((f16[1,520,128]{2,1,0:T(8,128)(2,1)S(1)}, f16[1,520,128]{2,1,0:T(8,128)(2,1)S(1)}, u32[]{:S(2)}, u32[]{:S(2)}) %collective-permute-start.34) | collective-permute-done | bytes 133152 | tf_op jit(solution)/shard_map/ppermute | solution.py:249
  140.2 0.8 fusion.5
  (98 shorter events, 4.0 us)
Async XLA Ops:
  0.0 11.1 %copy-start.1 = (bf16[512,128]{1,0:T(8,128)(2,1)S(1)}, bf16[512,128]{1,0:T(8,128)(2,1)}, u32[]{:S(2)}) copy-start(bf16[512,128]{1,0:T(8,128)(2,1)} %param.4) | copy-start | bytes 393220
  0.0 12.6 %copy-start.2 = (s32[1,1,512]{2,1,0:T(1,128)S(1)}, s32[1,1,512]{2,1,0:T(1,128)}, u32[]{:S(2)}) copy-start(s32[1,1,512]{2,1,0:T(1,128)} %param.7) | copy-start | bytes 6148
  0.0 12.7 %copy-start = (s32[1,1,65]{2,1,0:T(1,128)S(1)}, s32[1,1,65]{2,1,0:T(1,128)}, u32[]{:S(2)}) copy-start(s32[1,1,65]{2,1,0:T(1,128)} %param.6) | copy-start | bytes 784
  0.0 7.7 %collective-permute-start.2 = (bf16[512,128]{1,0:T(8,128)(2,1)}, bf16[512,128]{1,0:T(8,128)(2,1)S(1)}, u32[]{:S(2)}, u32[]{:S(2)}) collective-permute-start(bf16[512,128]{1,0:T(8,128)(2,1)} %param.4), channel_id=1, source_target_pairs={{0,64},{16,80},{32,96},{48,112},{64,0},{80,16},{96,32},{112,48},{1... | collective-permute-start | bytes 393224 | tf_op jit(solution)/shard_map/ppermute | solution.py:240
  4.0 5.2 %collective-permute-start = (bf16[512,128]{1,0:T(8,128)(2,1)}, bf16[512,128]{1,0:T(8,128)(2,1)S(1)}, u32[]{:S(2)}, u32[]{:S(2)}) collective-permute-start(bf16[512,128]{1,0:T(8,128)(2,1)} %param.4), channel_id=1, source_target_pairs={{0,16},{16,32},{32,48},{48,0},{64,80},{80,96},{96,112},{112,64},{1... | collective-permute-start | bytes 393224 | tf_op jit(solution)/shard_map/ppermute | solution.py:240
  4.4 6.4 %collective-permute-start.1 = (bf16[512,128]{1,0:T(8,128)(2,1)}, bf16[512,128]{1,0:T(8,128)(2,1)S(1)}, u32[]{:S(2)}, u32[]{:S(2)}) collective-permute-start(bf16[512,128]{1,0:T(8,128)(2,1)} %param.4), channel_id=1, source_target_pairs={{0,48},{16,0},{32,16},{48,32},{64,112},{80,64},{96,80},{112,96},{1... | collective-permute-start | bytes 393224 | tf_op jit(solution)/shard_map/ppermute | solution.py:240
  10.9 8.0 %collective-permute-start.3 = (bf16[1024,128]{1,0:T(8,128)(2,1)S(1)}, bf16[1024,128]{1,0:T(8,128)(2,1)S(1)}, u32[]{:S(2)}, u32[]{:S(2)}) collective-permute-start(bf16[1024,128]{1,0:T(8,128)(2,1)S(1)} %get-tuple-element.33.after_ref), channel_id=1, source_target_pairs={{0,64},{16,80},{32,96},{48,112},{64,0},{80,16},{96,32},{112,48},{1... | collective-permute-start | bytes 786440 | tf_op jit(solution)/shard_map/ppermute | solution.py:240
  11.1 8.5 %collective-permute-start.4 = (bf16[1024,128]{1,0:T(8,128)(2,1)S(1)}, bf16[1024,128]{1,0:T(8,128)(2,1)S(1)}, u32[]{:S(2)}, u32[]{:S(2)}) collective-permute-start(bf16[1024,128]{1,0:T(8,128)(2,1)S(1)} %pad_maximum_fusion.3), channel_id=1, source_target_pairs={{0,32},{16,48},{32,0},{48,16},{64,96},{80,112},{96,64},{112,80},{1... | collective-permute-start | bytes 786440 | tf_op jit(solution)/shard_map/ppermute | solution.py:240
  23.0 2.7 %collective-permute-start.6 = (f32[16,128,128]{2,1,0:T(8,128)S(1)}, f32[16,128,128]{2,1,0:T(8,128)S(1)}, u32[]{:S(2)}, u32[]{:S(2)}) collective-permute-start(f32[16,128,128]{2,1,0:T(8,128)S(1)} %get-tuple-element.12), channel_id=1, source_target_pairs={{0,1},{1,0},{2,3},{3,2},{4,5},{5,4},{6,7},{7,6},{8,9},{9,8},{10,11... | collective-permute-start | bytes 3145736 | tf_op jit(solution)/shard_map/ppermute | solution.py:273
  26.2 13.8 %collective-permute-start.7 = (f16[2,520,128]{2,1,0:T(8,128)(2,1)S(1)}, f16[2,520,128]{2,1,0:T(8,128)(2,1)S(1)}, u32[]{:S(2)}, u32[]{:S(2)}) collective-permute-start(f16[2,520,128]{2,1,0:T(8,128)(2,1)S(1)} %get-tuple-element.30), channel_id=1, source_target_pairs={{0,4},{1,5},{2,6},{3,7},{4,0},{5,1},{6,2},{7,3},{8,12},{9,13},{10,... | collective-permute-start | bytes 798728 | tf_op jit(solution)/shard_map/ppermute | solution.py:249
  35.5 6.4 %collective-permute-start.8 = (f16[2,520,128]{2,1,0:T(8,128)(2,1)S(1)}, f16[2,520,128]{2,1,0:T(8,128)(2,1)S(1)}, u32[]{:S(2)}, u32[]{:S(2)}) collective-permute-start(f16[2,520,128]{2,1,0:T(8,128)(2,1)S(1)} %get-tuple-element.31), channel_id=1, source_target_pairs={{0,8},{1,9},{2,10},{3,11},{4,12},{5,13},{6,14},{7,15},{8,0},{9,1},... | collective-permute-start | bytes 798728 | tf_op jit(solution)/shard_map/ppermute | solution.py:249
  36.8 5.3 %collective-permute-start.5 = (f32[16,128,128]{2,1,0:T(8,128)S(1)}, f32[16,128,128]{2,1,0:T(8,128)S(1)}, u32[]{:S(2)}, u32[]{:S(2)}) collective-permute-start(f32[16,128,128]{2,1,0:T(8,128)S(1)} %some_terms.12), channel_id=1, source_target_pairs={{0,1},{1,0},{2,3},{3,2},{4,5},{5,4},{6,7},{7,6},{8,9},{9,8},{10,11... | collective-permute-start | bytes 3145736 | tf_op jit(solution)/shard_map/ppermute | solution.py:279
  42.7 5.1 %collective-permute-start.11 = (f16[1,520,128]{2,1,0:T(8,128)(2,1)S(1)}, f16[1,520,128]{2,1,0:T(8,128)(2,1)S(1)}, u32[]{:S(2)}, u32[]{:S(2)}) collective-permute-start(f16[1,520,128]{2,1,0:T(8,128)(2,1)S(1)} %get-tuple-element.28), channel_id=1, source_target_pairs={{0,6},{1,7},{2,0},{3,1},{4,2},{5,3},{6,4},{7,5},{8,14},{9,15},{10,... | collective-permute-start | bytes 399368 | tf_op jit(solution)/shard_map/ppermute | solution.py:249
  42.8 6.3 %collective-permute-start.10 = (f16[1,520,128]{2,1,0:T(8,128)(2,1)S(1)}, f16[1,520,128]{2,1,0:T(8,128)(2,1)S(1)}, u32[]{:S(2)}, u32[]{:S(2)}) collective-permute-start(f16[1,520,128]{2,1,0:T(8,128)(2,1)S(1)} %get-tuple-element.29), channel_id=1, source_target_pairs={{0,2},{1,3},{2,4},{3,5},{4,6},{5,7},{6,0},{7,1},{8,10},{9,11},{10,... | collective-permute-start | bytes 399368 | tf_op jit(solution)/shard_map/ppermute | solution.py:249
  44.8 5.0 %collective-permute-start.9 = (f16[1,520,128]{2,1,0:T(8,128)(2,1)S(1)}, f16[1,520,128]{2,1,0:T(8,128)(2,1)S(1)}, u32[]{:S(2)}, u32[]{:S(2)}) collective-permute-start(f16[1,520,128]{2,1,0:T(8,128)(2,1)S(1)} %get-tuple-element.27), channel_id=1, source_target_pairs={{0,8},{1,9},{2,10},{3,11},{4,12},{5,13},{6,14},{7,15},{8,0},{9,1},... | collective-permute-start | bytes 399368 | tf_op jit(solution)/shard_map/ppermute | solution.py:249
  49.9 6.6 %collective-permute-start.12 = (bf16[512,128]{1,0:T(8,128)(2,1)S(1)}, bf16[512,128]{1,0:T(8,128)(2,1)S(1)}, u32[]{:S(2)}, u32[]{:S(2)}) collective-permute-start(bf16[512,128]{1,0:T(8,128)(2,1)S(1)} %get-tuple-element.16), channel_id=1, source_target_pairs={{0,64},{16,80},{32,96},{48,112},{64,0},{80,16},{96,32},{112,48},{1... | collective-permute-start | bytes 393224 | tf_op jit(solution)/shard_map/ppermute | solution.py:240
  53.3 5.3 %collective-permute-start.13 = (bf16[512,128]{1,0:T(8,128)(2,1)S(1)}, bf16[512,128]{1,0:T(8,128)(2,1)S(1)}, u32[]{:S(2)}, u32[]{:S(2)}) collective-permute-start(bf16[512,128]{1,0:T(8,128)(2,1)S(1)} %get-tuple-element.16), channel_id=1, source_target_pairs={{0,16},{16,32},{32,48},{48,0},{64,80},{80,96},{96,112},{112,64},{1... | collective-permute-start | bytes 393224 | tf_op jit(solution)/shard_map/ppermute | solution.py:240
  53.3 8.0 %collective-permute-start.14 = (bf16[512,128]{1,0:T(8,128)(2,1)S(1)}, bf16[512,128]{1,0:T(8,128)(2,1)S(1)}, u32[]{:S(2)}, u32[]{:S(2)}) collective-permute-start(bf16[512,128]{1,0:T(8,128)(2,1)S(1)} %get-tuple-element.16), channel_id=1, source_target_pairs={{0,48},{16,0},{32,16},{48,32},{64,112},{80,64},{96,80},{112,96},{1... | collective-permute-start | bytes 393224 | tf_op jit(solution)/shard_map/ppermute | solution.py:240
  56.4 12.9 %collective-permute-start.16 = (bf16[1024,128]{1,0:T(8,128)(2,1)S(1)}, bf16[1024,128]{1,0:T(8,128)(2,1)S(1)}, u32[]{:S(2)}, u32[]{:S(2)}) collective-permute-start(bf16[1024,128]{1,0:T(8,128)(2,1)S(1)} %pad_maximum_fusion.5), channel_id=1, source_target_pairs={{0,32},{16,48},{32,0},{48,16},{64,96},{80,112},{96,64},{112,80},{1... | collective-permute-start | bytes 786440 | tf_op jit(solution)/shard_map/ppermute | solution.py:240
  61.4 8.0 %collective-permute-start.15 = (bf16[1024,128]{1,0:T(8,128)(2,1)S(1)}, bf16[1024,128]{1,0:T(8,128)(2,1)S(1)}, u32[]{:S(2)}, u32[]{:S(2)}) collective-permute-start(bf16[1024,128]{1,0:T(8,128)(2,1)S(1)} %pad_maximum_fusion.4), channel_id=1, source_target_pairs={{0,64},{16,80},{32,96},{48,112},{64,0},{80,16},{96,32},{112,48},{1... | collective-permute-start | bytes 786440 | tf_op jit(solution)/shard_map/ppermute | solution.py:240
  70.7 2.8 %collective-permute-start.18 = (f32[16,128,128]{2,1,0:T(8,128)S(1)}, f32[16,128,128]{2,1,0:T(8,128)S(1)}, u32[]{:S(2)}, u32[]{:S(2)}) collective-permute-start(f32[16,128,128]{2,1,0:T(8,128)S(1)} %some_terms.17), channel_id=1, source_target_pairs={{0,1},{1,0},{2,3},{3,2},{4,5},{5,4},{6,7},{7,6},{8,9},{9,8},{10,11... | collective-permute-start | bytes 3145736 | tf_op jit(solution)/shard_map/ppermute | solution.py:273
  74.1 10.4 %collective-permute-start.19 = (f16[2,520,128]{2,1,0:T(8,128)(2,1)S(1)}, f16[2,520,128]{2,1,0:T(8,128)(2,1)S(1)}, u32[]{:S(2)}, u32[]{:S(2)}) collective-permute-start(f16[2,520,128]{2,1,0:T(8,128)(2,1)S(1)} %get-tuple-element.25), channel_id=1, source_target_pairs={{0,4},{1,5},{2,6},{3,7},{4,0},{5,1},{6,2},{7,3},{8,12},{9,13},{10,... | collective-permute-start | bytes 798728 | tf_op jit(solution)/shard_map/ppermute | solution.py:249
  78.1 7.8 %collective-permute-start.20 = (f16[2,520,128]{2,1,0:T(8,128)(2,1)S(1)}, f16[2,520,128]{2,1,0:T(8,128)(2,1)S(1)}, u32[]{:S(2)}, u32[]{:S(2)}) collective-permute-start(f16[2,520,128]{2,1,0:T(8,128)(2,1)S(1)} %get-tuple-element.26), channel_id=1, source_target_pairs={{0,8},{1,9},{2,10},{3,11},{4,12},{5,13},{6,14},{7,15},{8,0},{9,1},... | collective-permute-start | bytes 798728 | tf_op jit(solution)/shard_map/ppermute | solution.py:249
  80.4 5.7 %collective-permute-start.17 = (f32[16,128,128]{2,1,0:T(8,128)S(1)}, f32[16,128,128]{2,1,0:T(8,128)S(1)}, u32[]{:S(2)}, u32[]{:S(2)}) collective-permute-start(f32[16,128,128]{2,1,0:T(8,128)S(1)} %some_terms.15), channel_id=1, source_target_pairs={{0,1},{1,0},{2,3},{3,2},{4,5},{5,4},{6,7},{7,6},{8,9},{9,8},{10,11... | collective-permute-start | bytes 3145736 | tf_op jit(solution)/shard_map/ppermute | solution.py:279
  86.6 6.2 %collective-permute-start.23 = (f16[1,520,128]{2,1,0:T(8,128)(2,1)S(1)}, f16[1,520,128]{2,1,0:T(8,128)(2,1)S(1)}, u32[]{:S(2)}, u32[]{:S(2)}) collective-permute-start(f16[1,520,128]{2,1,0:T(8,128)(2,1)S(1)} %get-tuple-element.23), channel_id=1, source_target_pairs={{0,6},{1,7},{2,0},{3,1},{4,2},{5,3},{6,4},{7,5},{8,14},{9,15},{10,... | collective-permute-start | bytes 399368 | tf_op jit(solution)/shard_map/ppermute | solution.py:249
  90.3 6.2 %collective-permute-start.22 = (f16[1,520,128]{2,1,0:T(8,128)(2,1)S(1)}, f16[1,520,128]{2,1,0:T(8,128)(2,1)S(1)}, u32[]{:S(2)}, u32[]{:S(2)}) collective-permute-start(f16[1,520,128]{2,1,0:T(8,128)(2,1)S(1)} %get-tuple-element.24), channel_id=1, source_target_pairs={{0,2},{1,3},{2,4},{3,5},{4,6},{5,7},{6,0},{7,1},{8,10},{9,11},{10,... | collective-permute-start | bytes 399368 | tf_op jit(solution)/shard_map/ppermute | solution.py:249
  90.3 6.2 %collective-permute-start.21 = (f16[1,520,128]{2,1,0:T(8,128)(2,1)S(1)}, f16[1,520,128]{2,1,0:T(8,128)(2,1)S(1)}, u32[]{:S(2)}, u32[]{:S(2)}) collective-permute-start(f16[1,520,128]{2,1,0:T(8,128)(2,1)S(1)} %get-tuple-element.22), channel_id=1, source_target_pairs={{0,8},{1,9},{2,10},{3,11},{4,12},{5,13},{6,14},{7,15},{8,0},{9,1},... | collective-permute-start | bytes 399368 | tf_op jit(solution)/shard_map/ppermute | solution.py:249
  96.6 6.6 %collective-permute-start.24 = (bf16[512,128]{1,0:T(8,128)(2,1)S(1)}, bf16[512,128]{1,0:T(8,128)(2,1)S(1)}, u32[]{:S(2)}, u32[]{:S(2)}) collective-permute-start(bf16[512,128]{1,0:T(8,128)(2,1)S(1)} %get-tuple-element.14), channel_id=1, source_target_pairs={{0,64},{16,80},{32,96},{48,112},{64,0},{80,16},{96,32},{112,48},{1... | collective-permute-start | bytes 393224 | tf_op jit(solution)/shard_map/ppermute | solution.py:240
  96.7 6.6 %collective-permute-start.25 = (bf16[512,128]{1,0:T(8,128)(2,1)S(1)}, bf16[512,128]{1,0:T(8,128)(2,1)S(1)}, u32[]{:S(2)}, u32[]{:S(2)}) collective-permute-start(bf16[512,128]{1,0:T(8,128)(2,1)S(1)} %get-tuple-element.14), channel_id=1, source_target_pairs={{0,16},{16,32},{32,48},{48,0},{64,80},{80,96},{96,112},{112,64},{1... | collective-permute-start | bytes 393224 | tf_op jit(solution)/shard_map/ppermute | solution.py:240
  96.8 6.5 %collective-permute-start.26 = (bf16[512,128]{1,0:T(8,128)(2,1)S(1)}, bf16[512,128]{1,0:T(8,128)(2,1)S(1)}, u32[]{:S(2)}, u32[]{:S(2)}) collective-permute-start(bf16[512,128]{1,0:T(8,128)(2,1)S(1)} %get-tuple-element.14), channel_id=1, source_target_pairs={{0,48},{16,0},{32,16},{48,32},{64,112},{80,64},{96,80},{112,96},{1... | collective-permute-start | bytes 393224 | tf_op jit(solution)/shard_map/ppermute | solution.py:240
  103.2 13.3 %collective-permute-start.28 = (bf16[1024,128]{1,0:T(8,128)(2,1)S(1)}, bf16[1024,128]{1,0:T(8,128)(2,1)S(1)}, u32[]{:S(2)}, u32[]{:S(2)}) collective-permute-start(bf16[1024,128]{1,0:T(8,128)(2,1)S(1)} %pad_maximum_fusion.7), channel_id=1, source_target_pairs={{0,32},{16,48},{32,0},{48,16},{64,96},{80,112},{96,64},{112,80},{1... | collective-permute-start | bytes 786440 | tf_op jit(solution)/shard_map/ppermute | solution.py:240
  103.3 13.1 %collective-permute-start.27 = (bf16[1024,128]{1,0:T(8,128)(2,1)S(1)}, bf16[1024,128]{1,0:T(8,128)(2,1)S(1)}, u32[]{:S(2)}, u32[]{:S(2)}) collective-permute-start(bf16[1024,128]{1,0:T(8,128)(2,1)S(1)} %pad_maximum_fusion.6), channel_id=1, source_target_pairs={{0,64},{16,80},{32,96},{48,112},{64,0},{80,16},{96,32},{112,48},{1... | collective-permute-start | bytes 786440 | tf_op jit(solution)/shard_map/ppermute | solution.py:240
  117.9 2.7 %collective-permute-start.30 = (f32[16,128,128]{2,1,0:T(8,128)S(1)}, f32[16,128,128]{2,1,0:T(8,128)S(1)}, u32[]{:S(2)}, u32[]{:S(2)}) collective-permute-start(f32[16,128,128]{2,1,0:T(8,128)S(1)} %some_terms.21), channel_id=1, source_target_pairs={{0,1},{1,0},{2,3},{3,2},{4,5},{5,4},{6,7},{7,6},{8,9},{9,8},{10,11... | collective-permute-start | bytes 3145736 | tf_op jit(solution)/shard_map/ppermute | solution.py:273
  121.1 10.3 %collective-permute-start.31 = (f16[2,520,128]{2,1,0:T(8,128)(2,1)S(1)}, f16[2,520,128]{2,1,0:T(8,128)(2,1)S(1)}, u32[]{:S(2)}, u32[]{:S(2)}) collective-permute-start(f16[2,520,128]{2,1,0:T(8,128)(2,1)S(1)} %get-tuple-element.20), channel_id=1, source_target_pairs={{0,4},{1,5},{2,6},{3,7},{4,0},{5,1},{6,2},{7,3},{8,12},{9,13},{10,... | collective-permute-start | bytes 798728 | tf_op jit(solution)/shard_map/ppermute | solution.py:249
  121.4 10.0 %collective-permute-start.32 = (f16[2,520,128]{2,1,0:T(8,128)(2,1)S(1)}, f16[2,520,128]{2,1,0:T(8,128)(2,1)S(1)}, u32[]{:S(2)}, u32[]{:S(2)}) collective-permute-start(f16[2,520,128]{2,1,0:T(8,128)(2,1)S(1)} %get-tuple-element.21), channel_id=1, source_target_pairs={{0,8},{1,9},{2,10},{3,11},{4,12},{5,13},{6,14},{7,15},{8,0},{9,1},... | collective-permute-start | bytes 798728 | tf_op jit(solution)/shard_map/ppermute | solution.py:249
  123.4 8.2 %collective-permute-start.29 = (f32[16,128,128]{2,1,0:T(8,128)S(1)}, f32[16,128,128]{2,1,0:T(8,128)S(1)}, u32[]{:S(2)}, u32[]{:S(2)}) collective-permute-start(f32[16,128,128]{2,1,0:T(8,128)S(1)} %some_terms.19), channel_id=1, source_target_pairs={{0,1},{1,0},{2,3},{3,2},{4,5},{5,4},{6,7},{7,6},{8,9},{9,8},{10,11... | collective-permute-start | bytes 3145736 | tf_op jit(solution)/shard_map/ppermute | solution.py:279
  132.1 5.2 %collective-permute-start.35 = (f16[1,520,128]{2,1,0:T(8,128)(2,1)S(1)}, f16[1,520,128]{2,1,0:T(8,128)(2,1)S(1)}, u32[]{:S(2)}, u32[]{:S(2)}) collective-permute-start(f16[1,520,128]{2,1,0:T(8,128)(2,1)S(1)} %get-tuple-element.18), channel_id=1, source_target_pairs={{0,6},{1,7},{2,0},{3,1},{4,2},{5,3},{6,4},{7,5},{8,14},{9,15},{10,... | collective-permute-start | bytes 399368 | tf_op jit(solution)/shard_map/ppermute | solution.py:249
  133.9 6.2 %collective-permute-start.34 = (f16[1,520,128]{2,1,0:T(8,128)(2,1)S(1)}, f16[1,520,128]{2,1,0:T(8,128)(2,1)S(1)}, u32[]{:S(2)}, u32[]{:S(2)}) collective-permute-start(f16[1,520,128]{2,1,0:T(8,128)(2,1)S(1)} %get-tuple-element.19), channel_id=1, source_target_pairs={{0,2},{1,3},{2,4},{3,5},{4,6},{5,7},{6,0},{7,1},{8,10},{9,11},{10,... | collective-permute-start | bytes 399368 | tf_op jit(solution)/shard_map/ppermute | solution.py:249
  134.2 5.9 %collective-permute-start.33 = (f16[1,520,128]{2,1,0:T(8,128)(2,1)S(1)}, f16[1,520,128]{2,1,0:T(8,128)(2,1)S(1)}, u32[]{:S(2)}, u32[]{:S(2)}) collective-permute-start(f16[1,520,128]{2,1,0:T(8,128)(2,1)S(1)} %get-tuple-element.17), channel_id=1, source_target_pairs={{0,8},{1,9},{2,10},{3,11},{4,12},{5,13},{6,14},{7,15},{8,0},{9,1},... | collective-permute-start | bytes 399368 | tf_op jit(solution)/shard_map/ppermute | solution.py:249
